TPU v7x, 128 devices: a whole 4x4x4 slice. The times are simulated.
128 devices in a mesh: row: 8 (over y, core), col: 16 (over x, z).
Axes of the slice: x: 4, y: 4, z: 4, core: 2. Of those that a mesh axis runs over, the one named last changes fastest.
Arguments:
- activations: bfloat16 [1024, 8192], P('col', 'row')
- out_grads: bfloat16 [1024, 32768], P('row', 'col')
- queries: bfloat16 [4, 8192, 32768], P(None, 'row', 'col'), may hold values from -0.00036621094 to 0.00036621094
- seq_start: int32 [16], replicated, may hold values from 0 to 1008, as said below
- seq_len: int32 [16], replicated, may hold values from 16 to 64, as said below
Outputs:
- scores: float32 [4, 16], replicated
Inputs may be any that keep to these rules, and one draw needn't show every extreme that they name: `seq_start`: sequence s lies inside tokens s * 64 to (s + 1) * 64 - 1. `seq_len`: some sequence has exactly 64 tokens and some exactly 16.
All inputs are finite; a program needn't handle non-finite values.
Results may differ from a plain program's by a relative error of at most 0.0003.
Values may be sent and summed in bfloat16 or wider, within the bound.
No kernel may reach another device: no remote copies, remote signals or barrier semaphores. Data moves between devices by JAX's collectives and lax.ppermute only.
A program may use at most 192 MiB of HBM per device.

v0:
```python
import jax
import jax.numpy as jnp
from jax import lax
from jax.sharding import PartitionSpec as P


def membership(row_count, seq_start, seq_len):
    positions = jnp.arange(row_count, dtype=jnp.int32)
    seq_end = seq_start + seq_len
    inside = (positions[:, None] >= seq_start[None, :]) & (positions[:, None] < seq_end[None, :])
    return inside.astype(jnp.float32)


def token_scores(act_block, grad_block, queries):
    products = jnp.einsum("ti,qij->qtj", act_block, queries, preferred_element_type=jnp.float32)
    return jnp.sum(products * grad_block.astype(jnp.float32)[None], axis=2)


def gather_grads(out_grads):
    return lax.all_gather(out_grads, "row", axis=0, tiled=True)


def on_device(activations, out_grads, queries, seq_start, seq_len):
    highest = lax.Precision.HIGHEST
    act_all = lax.all_gather(activations, "col", axis=0, tiled=True)
    total_rows = act_all.shape[0]
    grad_all = gather_grads(out_grads)
    per_token = token_scores(act_all, grad_all, queries)
    member = membership(total_rows, seq_start, seq_len)
    partial_value = jnp.dot(per_token, member, precision=highest)
    return lax.psum(partial_value, ("row", "col"))


def solution(mesh):
    in_specs = (P("col", "row"), P("row", "col"), P(None, "row", "col"), P(), P())
    out_specs = P()
    return jax.shard_map(
        on_device, mesh=mesh, in_specs=in_specs, out_specs=out_specs, check_vma=False
    )
```

profile of v0, /device:TPU:0, one launch (start us, length us, event | category | flops | bytes accessed | tf_op | source)
XLA Modules:
  0.0 185.8 jit_solution(14050686330593222717)
XLA Ops:
  6.5 0.0 all-gather.5.cloned.1.call-start
  6.5 0.7 all-gather.5.cloned.1.call-update
  7.3 0.0 all-gather.3.cloned.1.call-start
  7.3 0.7 all-gather.3.cloned.1.call-update
  8.0 0.7 add.5
  8.7 35.0 %all-gather.5.cloned.1.call-done = bf16[1024,2048]{1,0:T(8,128)(2,1)} async-done(((bf16[128,2048]{1,0:T(8,128)(2,1)}), bf16[1024,2048]{1,0:T(8,128)(2,1)}) %all-gather.5.cloned.1.call-update) | async-done | bytes 4194320 | tf_op jit(solution)/shard_map/all_gather | solution.py:20
  43.7 6.9 %copy.7 = f32[1024,2048]{0,1:T(8,128)} copy(bf16[1024,2048]{1,0:T(8,128)(2,1)} %all-gather.5.cloned.1.call-done) | data formatting | bytes 12582912 | tf_op jit(solution)/shard_map/convert_element_type | solution.py:16
  50.6 0.0 copy-start
  50.6 40.5 %all-gather.3.cloned.1.call-done = bf16[1024,1024]{1,0:T(8,128)(2,1)} async-done(((bf16[64,1024]{1,0:T(8,128)(2,1)}), bf16[1024,1024]{1,0:T(8,128)(2,1)}) %all-gather.3.cloned.1.call-update) | async-done | bytes 2097168 | tf_op jit(solution)/shard_map/all_gather | solution.py:25
  91.1 23.2 %fusion = f32[4,1024]{1,0:T(4,128)S(1)} fusion(bf16[4,1024,2048]{2,1,0:T(8,128)(2,1)} %param.7, f32[1024,2048]{0,1:T(8,128)} %copy.7, bf16[1024,1024]{1,0:T(8,128)(2,1)} %all-gather.3.cloned.1.call-done), kind=kOutput, calls=%fused_computation.1 | convolution fusion | flops 17196642304 | bytes 27279360 | tf_op jit(solution)/shard_map/ti,qij->qtj/dot_general | solution.py:15
  114.3 0.0 copy-done
  114.3 0.3 fusion.3
  114.6 64.4 %psum.7 = f32[4,16]{1,0:T(4,128)} all-reduce(f32[4,16]{1,0:T(4,128)S(1)} %fusion.3), channel_id=1, replica_groups=mesh['row'=8,'col'=16] {'row','col'}, use_global_device_ids=true, to_apply=%region_1.0 | all-reduce | flops 64 | bytes 512 | tf_op jit(solution)/shard_map/psum | solution.py:31
Async XLA Ops:
  6.5 37.2 %all-gather.5.cloned.1.call-start = ((), (), s32[]{:S(2)}) async-start(), calls=%async_computation.1 | async-start | bytes 4718592 | tf_op jit(solution)/shard_map/all_gather | solution.py:20
  7.3 83.8 %all-gather.3.cloned.1.call-start = ((), (), s32[]{:S(2)}) async-start(), calls=%async_computation | async-start | bytes 2228224 | tf_op jit(solution)/shard_map/all_gather | solution.py:25
  50.6 63.7 %copy-start = (s32[16]{0:T(128)S(1)}, s32[16]{0:T(128)}, u32[]{:S(2)}) copy-start(s32[16]{0:T(128)} %param.8) | copy-start | bytes 196
Sparse Core Ops, SparseCore 0:
  9.1 34.5 all-gather.4
  45.8 45.1 all-gather.2
where the time goes:
time: 187 us; the launch traced here: 186 us
  waiting for transfers between devices  76.9 us (41%)
  blocking collectives  64.4 us (34%)
  matrix products  23.5 us (13%)
  between operations  13.4 us (7%)
  local copies, waits for them, and re-layouts  6.88 us (4%)
    psum x1, blocking collectives, on_device(): return lax.psum(partial_value, ('row', 'col'))  64.4 us
    all_gather x1, waiting for transfers between devices, on_device(): act_all = lax.all_gather(activations, 'col', axis=0, tiled=True)  40.5 us
    all_gather x1, waiting for transfers between devices, gather_grads(): return lax.all_gather(out_grads, 'row', axis=0, tiled=True)  35 us
    dot_general x1, matrix products, token_scores(): jnp.einsum('ti,qij->qtj', act_block, queries, preferred_element_type=jnp....  23.2 us
    convert_element_type x1, local copies, waits for them, and re-layouts, token_scores(): return jnp.sum(products * grad_block.astype(jnp.float32)[None], axis=2)  6.87 us
  transfers between devices with their start and end apart: 2, of which 2 were waited for; matrix products, arithmetic and copies ran while one was open for 4% of the time, Pallas kernels for 0%

commit v1 on v0

v1 whole, which is shorter than its diff:
```python
import functools

import jax
import jax.numpy as jnp
from jax import lax
from jax.experimental import pallas as pl
from jax.experimental.pallas import tpu as pltpu
from jax.sharding import PartitionSpec as P

NT = (((1,), (1,)), ((), ()))
SLOT = 64
VMEM = pl.BlockSpec(memory_space=pltpu.VMEM)
SMEM = pl.BlockSpec(memory_space=pltpu.SMEM)
ANY = pl.BlockSpec(memory_space=pl.ANY)


def along_y(shift):
    return [(i, ((i // 2 + shift) % 4) * 2 + i % 2) for i in range(8)]


def along_z(shift):
    return [(i, (i // 4) * 4 + (i + shift) % 4) for i in range(16)]


def along_x(shift):
    return [(i, (i + 4 * shift) % 16) for i in range(16)]


OTHER_CORE = [(i, i ^ 1) for i in range(8)]


def first_row(place):
    dy, dcore, row = place
    index = lax.axis_index("row")
    y, core = index // 2, index % 2
    return pl.multiple_of((y + dy) % 4 * 256 + (core + dcore) % 2 * 128 + row, SLOT)


def multiply(places, blocks, rows, query, products, q):
    start = 0
    for block in blocks:
        rows[start : start + block.shape[0], :] = block[...]
        start += block.shape[0]

    result = lax.dot_general(rows[...], query, NT, preferred_element_type=jnp.float32)
    start = 0
    for place, block in zip(places, blocks, strict=True):
        count = block.shape[0]
        products[q, pl.ds(first_row(place), count), :] = result[start : start + count]
        start += count


def first_kernel(places, *refs):
    n = len(places)
    blocks, queries, products, held, rows, sems = refs[:n], refs[n], *refs[n + 1 :]
    copies = [pltpu.make_async_copy(queries.at[q], held.at[q], sems.at[q]) for q in range(queries.shape[0])]
    for copy in copies:
        copy.start()
    for q, copy in enumerate(copies):
        copy.wait()
        multiply(places, blocks, rows, held[q], products, q)


def next_kernel(places, *refs):
    n = len(places)
    blocks, held, _, products, rows = refs[:n], refs[n], *refs[n + 1 :]

    def one_query(q, carry):
        multiply(places, blocks, rows, held[q], products, q)
        return carry

    lax.fori_loop(0, held.shape[0], one_query, 0)


def params(limit):
    return pltpu.CompilerParams(vmem_limit_bytes=limit << 20)


def cost(blocks, queries):
    rows = sum(b.shape[0] for b in blocks)
    return pl.CostEstimate(flops=2 * rows * queries.size, bytes_accessed=2 * queries.size, transcendentals=0)


def first_products(name, places, blocks, queries, tokens):
    nq, width, depth = queries.shape
    rows = sum(b.shape[0] for b in blocks)
    return pl.pallas_call(
        functools.partial(first_kernel, places),
        in_specs=[VMEM] * len(blocks) + [ANY],
        out_specs=[VMEM, VMEM],
        out_shape=[pltpu.VMEM((nq, tokens, width), jnp.float32), pltpu.VMEM(queries.shape, queries.dtype)],
        scratch_shapes=[pltpu.VMEM((rows, depth), jnp.bfloat16), pltpu.SemaphoreType.DMA((nq,))],
        compiler_params=params(8),
        cost_estimate=cost(blocks, queries),
        name=name,
    )(*blocks, queries)


def next_products(name, places, blocks, held, products):
    rows = sum(b.shape[0] for b in blocks)
    n = len(blocks)
    return pl.pallas_call(
        functools.partial(next_kernel, places),
        in_specs=[VMEM] * (n + 2),
        out_specs=VMEM,
        out_shape=pltpu.VMEM(products.shape, products.dtype),
        input_output_aliases={n + 1: 0},
        scratch_shapes=[pltpu.VMEM((rows, held.shape[2]), jnp.bfloat16)],
        compiler_params=params(8),
        cost_estimate=cost(blocks, held),
        name=name,
    )(*blocks, held, products)


def score_kernel(seq_start, seq_len, own, ahead, far, behind, products, out, lanes):
    col = lax.axis_index("col")
    x, z = col // 4, col % 4
    nq = out.shape[0]
    width = products.shape[2]
    position = lax.broadcasted_iota(jnp.int32, (SLOT, 1), 0)
    for dx, block in enumerate((own, ahead, far, behind)):

        def one_slot(dz, carry, dx=dx, block=block):
            slot = (x + dx) % 4 * 4 + (z + dz) % 4
            base = pl.multiple_of(slot * SLOT, SLOT)
            token = position + base
            start = seq_start[slot]
            inside = (token >= start) & (token < start + seq_len[slot])
            totals = [jnp.zeros((SLOT, 128), jnp.float32) for _ in range(nq)]
            for i in range(0, width, 128):
                act = block[dz, :, i : i + 128].astype(jnp.float32)
                for q in range(nq):
                    totals[q] += products[q, pl.ds(base, SLOT), i : i + 128] * act
            for q in range(nq):
                kept = jnp.where(inside, totals[q], 0.0)
                lanes[q, pl.ds(slot, 1), :] = jnp.sum(kept, axis=0, keepdims=True)
            return carry

        lax.fori_loop(0, 4, one_slot, 0)
    ones = jnp.ones((8, 128), jnp.float32)
    for q in range(nq):
        sums = lax.dot_general(ones, lanes[q], NT, precision=lax.Precision.HIGHEST, preferred_element_type=jnp.float32)
        out[q : q + 1, :] = sums[:1, :]


def partial_scores(seq_start, seq_len, acts, products):
    nq = products.shape[0]
    nseq = seq_start.shape[0]
    return pl.pallas_call(
        score_kernel,
        in_specs=[SMEM] * 2 + [VMEM] * 5,
        out_specs=VMEM,
        out_shape=jax.ShapeDtypeStruct((nq, nseq), jnp.float32),
        scratch_shapes=[pltpu.VMEM((nq, nseq, 128), jnp.float32)],
        compiler_params=params(8),
        cost_estimate=pl.CostEstimate(flops=1 << 30, bytes_accessed=4 << 20, transcendentals=0),
        name="scores",
    )(seq_start, seq_len, *acts, products)


def everywhere(value, axis, size):
    copies = jnp.broadcast_to(value[None], (size,) + value.shape)
    return jnp.sum(lax.all_to_all(copies, axis, 0, 0, tiled=True), axis=0)


def on_device(activations, out_grads, queries, seq_start, seq_len):
    half = out_grads.shape[0] // 2
    tokens = SLOT * seq_start.shape[0]

    def to_core(block):
        return lax.ppermute(block, "row", OTHER_CORE)

    def rows_of_z(block):
        parts = [block] + [lax.ppermute(block, "col", along_z(-d)) for d in (1, 2, 3)]
        return jnp.stack(parts)

    from_below = lax.ppermute(out_grads, "row", along_y(1))
    from_above = lax.ppermute(out_grads, "row", along_y(-1))
    products, held = first_products(
        "near", [(0, 0, 0), (0, 1, 0)], [out_grads, to_core(out_grads)], queries, tokens
    )

    far_one = lax.ppermute(activations, "col", along_x(2))
    own = rows_of_z(activations)
    far_act = rows_of_z(far_one)
    ahead = lax.ppermute(own, "col", along_x(-1))
    behind = lax.ppermute(own, "col", along_x(1))

    far_first = lax.ppermute(from_below[:half], "row", along_y(1))
    far_second = lax.ppermute(from_above[half:], "row", along_y(-1))
    products = next_products("mid", [(3, 0, 0), (1, 0, 0)], [from_below, from_above], held, products)
    products = next_products(
        "mid_core", [(3, 1, 0), (1, 1, 0)], [to_core(from_below), to_core(from_above)], held, products
    )
    products = next_products(
        "far",
        [(2, 0, 0), (2, 0, half), (2, 1, 0), (2, 1, half)],
        [far_first, far_second, to_core(far_first), to_core(far_second)],
        held,
        products,
    )
    scores = partial_scores(seq_start, seq_len, [own, ahead, far_act, behind], products)
    scores = everywhere(scores, "row", lax.axis_size("row"))
    return everywhere(scores, "col", lax.axis_size("col"))


def solution(mesh):
    in_specs = (P("col", "row"), P("row", "col"), P(None, "row", "col"), P(), P())
    return jax.shard_map(on_device, mesh=mesh, in_specs=in_specs, out_specs=P(), check_vma=False)
```

time: 187 us -> 86.9 us (0.46)
  waiting for transfers between devices: 76.9 us -> 18 us
  blocking collectives: 64.4 us -> 17.9 us
  Pallas kernels: 0 us -> 25.2 us
  matrix products: 23.5 us -> 0 us
  starting transfers between devices: 0.04 us -> 22.7 us
  between operations: 13.4 us -> 0.13 us
  local copies, waits for them, and re-layouts: 6.88 us -> 1.11 us
    all_gather x2 -> x0, waiting for transfers between devices: 75.5 us -> none  [the longest x1 40.5 us: on_device(): act_all = lax.all_gather(activations, 'col', axis=0, tiled=True)]
    psum x1 -> x0, blocking collectives: 64.4 us -> none  [on_device(): return lax.psum(partial_value, ('row', 'col'))]
    pallas_call x0 -> x5, Pallas kernels: none -> 25.2 us  [the longest x3 15.4 us: next_products(): pl.pallas_call(functools.partial(next_kernel, places), in_specs=[VMEM] *...]
    dot_general x2 -> x0, matrix products: 23.5 us -> none  [the longest x1 23.2 us: token_scores(): jnp.einsum('ti,qij->qtj', act_block, queries, preferred_element_type=jnp....]
    ppermute x0 -> x18, starting transfers between devices: none -> 22.7 us  [the longest x6 9.96 us: rows_of_z(): lax.ppermute(block, 'col', along_z(-d))]
    ppermute x0 -> x18, waiting for transfers between devices: none -> 18 us  [the longest x6 14.6 us: rows_of_z(): lax.ppermute(block, 'col', along_z(-d))]
    all_to_all x0 -> x2, blocking collectives: none -> 17.9 us  [everywhere(): return jnp.sum(lax.all_to_all(copies, axis, 0, 0, tiled=True), axis=0)]
    convert_element_type x1 -> x0, local copies, waits for them, and re-layouts: 6.87 us -> none  [token_scores(): return jnp.sum(products * grad_block.astype(jnp.float32)[None], axis=2)]
  transfers between devices with their start and end apart: 2 -> 18, of which waited for: 2 -> 6; matrix products, arithmetic and copies ran while one was open for 4% -> 1% of each run, Pallas kernels for 0% -> 26%
where the time goes in v1:
time: 86.9 us; the launch traced here: 86.7 us
  Pallas kernels  25.2 us (29%)
  starting transfers between devices  22.7 us (26%)
  waiting for transfers between devices  18 us (21%)
  blocking collectives  17.9 us (21%)
  other arithmetic  1.66 us (2%)
  local copies, waits for them, and re-layouts  1.11 us (1%)
    all_to_all x2, blocking collectives, everywhere(): return jnp.sum(lax.all_to_all(copies, axis, 0, 0, tiled=True), axis=0)  17.9 us
    pallas_call x3, Pallas kernels, next_products(): pl.pallas_call(functools.partial(next_kernel, places), in_specs=[VMEM] *...  15.4 us
    ppermute x6, waiting for transfers between devices, rows_of_z(): lax.ppermute(block, 'col', along_z(-d))  14.6 us
    ppermute x6, starting transfers between devices, rows_of_z(): lax.ppermute(block, 'col', along_z(-d))  9.96 us
    pallas_call x1, Pallas kernels, first_products(): pl.pallas_call(functools.partial(first_kernel, places), in_specs=[VMEM] *...  7.34 us
    ppermute x1, waiting for transfers between devices, on_device(): behind = lax.ppermute(own, 'col', along_x(1))  3.43 us
    ppermute x1, starting transfers between devices, on_device(): far_one = lax.ppermute(activations, 'col', along_x(2))  3.11 us
    ppermute x1, starting transfers between devices, on_device(): far_second = lax.ppermute(from_above[half:], 'row', along_y(-1))  2.96 us
  transfers between devices with their start and end apart: 18, of which 6 were waited for; matrix products, arithmetic and copies ran while one was open for 1% of the time, Pallas kernels for 26%

profile of v1, /device:TPU:0, one launch (start us, length us, event | category | flops | bytes accessed | tf_op | source)
XLA Modules:
  0.0 86.7 jit_solution(3417427587934392627)
XLA Ops:
  0.0 3.1 %collective-permute-start.4 = (bf16[64,1024]{1,0:T(8,128)(2,1)}, bf16[64,1024]{1,0:T(8,128)(2,1)S(1)}, u32[]{:S(2)}, u32[]{:S(2)}) collective-permute-start(bf16[64,1024]{1,0:T(8,128)(2,1)} %param.5), channel_id=1, source_target_pairs={{0,8},{1,9},{2,10},{3,11},{4,12},{5,13},{6,14},{7,15},{8,0},{9,1},... | collective-permute-start | bytes 393224 | tf_op jit(solution)/shard_map/ppermute | solution.py:183
  3.1 1.6 %collective-permute-start.9 = (bf16[128,2048]{1,0:T(8,128)(2,1)}, bf16[128,2048]{1,0:T(8,128)(2,1)S(1)}, u32[]{:S(2)}, u32[]{:S(2)}) collective-permute-start(bf16[128,2048]{1,0:T(8,128)(2,1)} %refs_0_.1), channel_id=1, source_target_pairs={{0,32},{16,48},{32,64},{48,80},{64,96},{80,112},{96,0},{112,16},{1... | collective-permute-start | bytes 1572872 | tf_op jit(solution)/shard_map/ppermute | solution.py:177
  4.7 1.7 %collective-permute-start.11 = (bf16[128,2048]{1,0:T(8,128)(2,1)}, bf16[128,2048]{1,0:T(8,128)(2,1)S(1)}, u32[]{:S(2)}, u32[]{:S(2)}) collective-permute-start(bf16[128,2048]{1,0:T(8,128)(2,1)} %refs_0_.1), channel_id=1, source_target_pairs={{0,96},{16,112},{32,0},{48,16},{64,32},{80,48},{96,64},{112,80},{1... | collective-permute-start | bytes 1572872 | tf_op jit(solution)/shard_map/ppermute | solution.py:178
  6.3 4.0 %collective-permute-start = (bf16[64,1024]{1,0:T(8,128)(2,1)}, bf16[64,1024]{1,0:T(8,128)(2,1)S(1)}, u32[]{:S(2)}, u32[]{:S(2)}) collective-permute-start(bf16[64,1024]{1,0:T(8,128)(2,1)} %param.5), channel_id=1, source_target_pairs={{0,3},{1,0},{2,1},{3,2},{4,7},{5,4},{6,5},{7,6},{8,11},{9,8},{10,9... | collective-permute-start | bytes 393224 | tf_op jit(solution)/shard_map/ppermute | solution.py:174
  10.4 0.5 collective-permute-start.1
  10.9 6.0 %collective-permute-done = bf16[64,1024]{1,0:T(8,128)(2,1)S(1)} collective-permute-done((bf16[64,1024]{1,0:T(8,128)(2,1)}, bf16[64,1024]{1,0:T(8,128)(2,1)S(1)}, u32[]{:S(2)}, u32[]{:S(2)}) %collective-permute-start) | collective-permute-done | bytes 131104 | tf_op jit(solution)/shard_map/ppermute | solution.py:174
  16.9 0.8 collective-permute-done.1
  17.7 2.8 %collective-permute-start.5 = (bf16[64,1024]{1,0:T(8,128)(2,1)S(1)}, bf16[64,1024]{1,0:T(8,128)(2,1)S(1)}, u32[]{:S(2)}, u32[]{:S(2)}) collective-permute-start(bf16[64,1024]{1,0:T(8,128)(2,1)S(1)} %collective-permute-done.4), channel_id=1, source_target_pairs={{0,3},{1,0},{2,1},{3,2},{4,7},{5,4},{6,5},{7,6},{8,11},{9,8},{10,9... | collective-permute-start | bytes 393224 | tf_op jit(solution)/shard_map/ppermute | solution.py:174
  20.5 3.6 %collective-permute-done.2 = bf16[64,1024]{1,0:T(8,128)(2,1)S(1)} collective-permute-done((bf16[64,1024]{1,0:T(8,128)(2,1)}, bf16[64,1024]{1,0:T(8,128)(2,1)S(1)}, u32[]{:S(2)}, u32[]{:S(2)}) %collective-permute-start.2) | collective-permute-done | bytes 131104 | tf_op jit(solution)/shard_map/ppermute | solution.py:174
  24.1 0.8 collective-permute-start.6
  25.0 1.8 %collective-permute-start.7 = (bf16[64,1024]{1,0:T(8,128)(2,1)S(1)}, bf16[64,1024]{1,0:T(8,128)(2,1)S(1)}, u32[]{:S(2)}, u32[]{:S(2)}) collective-permute-start(bf16[64,1024]{1,0:T(8,128)(2,1)S(1)} %collective-permute-done.4), channel_id=1, source_target_pairs={{0,1},{1,2},{2,3},{3,0},{4,5},{5,6},{6,7},{7,4},{8,9},{9,10},{10,1... | collective-permute-start | bytes 393224 | tf_op jit(solution)/shard_map/ppermute | solution.py:174
  26.7 1.0 %pad_maximum_fusion.own = bf16[4,64,1024]{2,1,0:T(8,128)(2,1)S(1)} fusion(bf16[1,64,1024]{2,1,0:T(8,128)(2,1)S(1)} %bitcast.13, bf16[1,64,1024]{2,1,0:T(8,128)(2,1)S(1)} %bitcast.11, bf16[1,64,1024]{2,1,0:T(8,128)(2,1)S(1)} %bitcast.10, bf16[1,64,1024]{2,1,0:T(8,128)(2,1)} %bitcast.8), kind=kLoop, calls=%fused_computation | loop fusion | flops 786432 | bytes 1048576 | tf_op jit(solution)/shard_map/stack | solution.py:175
  27.7 4.0 %collective-permute-done.6 = bf16[64,1024]{1,0:T(8,128)(2,1)S(1)} collective-permute-done((bf16[64,1024]{1,0:T(8,128)(2,1)S(1)}, bf16[64,1024]{1,0:T(8,128)(2,1)S(1)}, u32[]{:S(2)}, u32[]{:S(2)}) %collective-permute-start.6) | collective-permute-done | bytes 131104 | tf_op jit(solution)/shard_map/ppermute | solution.py:174
  31.7 1.1 %collective-permute-start.3 = (bf16[4,64,1024]{2,1,0:T(8,128)(2,1)S(1)}, bf16[4,64,1024]{2,1,0:T(8,128)(2,1)S(1)}, u32[]{:S(2)}, u32[]{:S(2)}) collective-permute-start(bf16[4,64,1024]{2,1,0:T(8,128)(2,1)S(1)} %pad_maximum_fusion.own), channel_id=1, source_target_pairs={{0,12},{1,13},{2,14},{3,15},{4,0},{5,1},{6,2},{7,3},{8,4},{9,5},{1... | collective-permute-start | bytes 1572872 | tf_op jit(solution)/shard_map/ppermute | solution.py:186
  32.8 0.1 collective-permute-done.7
  33.0 0.1 pad_maximum_fusion.1.far
  33.1 0.4 collective-permute-start.10
  33.5 3.0 %collective-permute-start.12 = (bf16[64,2048]{1,0:T(8,128)(2,1)S(1)}, bf16[64,2048]{1,0:T(8,128)(2,1)S(1)}, u32[]{:S(2)}, u32[]{:S(2)}) collective-permute-start(bf16[64,2048]{1,0:T(8,128)(2,1)S(1)} %slice.9), channel_id=1, source_target_pairs={{0,96},{16,112},{32,0},{48,16},{64,32},{80,48},{96,64},{112,80},{1... | collective-permute-start | bytes 786440 | tf_op jit(solution)/shard_map/ppermute | solution.py:190
  36.5 0.5 collective-permute-start.17
  37.0 1.0 %copy-done = bf16[128,2048]{1,0:T(8,128)(2,1)S(1)} copy-done((bf16[128,2048]{1,0:T(8,128)(2,1)S(1)}, bf16[128,2048]{1,0:T(8,128)(2,1)}, u32[]{:S(2)}) %copy-start) | copy-done | bytes 524312
  38.0 7.3 %near.1 = (f32[4,1024,1024]{2,1,0:T(8,128)S(1)}, bf16[4,1024,2048]{2,1,0:T(8,128)(2,1)S(1)}) custom-call(bf16[128,2048]{1,0:T(8,128)(2,1)S(1)} %copy-done, bf16[128,2048]{1,0:T(8,128)(2,1)S(1)} %collective-permute-done.15.refs_1_, bf16[4,1024,2048]{2,1,0:T(8,128)(2,1)} %refs_2_.1), custom_call_target="tpu_custom_call" | custom-call | flops 4294967296 | bytes 16777216 | tf_op jit(solution)/shard_map/near/pallas_call | solution.py:87
  45.4 5.1 %mid.1.refs_3_ = f32[4,1024,1024]{2,1,0:T(8,128)S(1)} custom-call(bf16[128,2048]{1,0:T(8,128)(2,1)S(1)} %collective-permute-done.9.refs_0_, bf16[128,2048]{1,0:T(8,128)(2,1)S(1)} %collective-permute-done.11.refs_1_, bf16[4,1024,2048]{2,1,0:T(8,128)(2,1)S(1)} %get-tuple-element.7.refs_2_.refs_4_, ...), custom_call_target="tpu_custom_call", output_to_operand_aliasing={{}: (3, {})} | custom-call | flops 4294967296 | bytes 16777216 | tf_op jit(solution)/shard_map/mid/pallas_call | solution.py:102
  50.5 0.9 collective-permute-start.8
  51.4 0.5 collective-permute-start.14
  51.9 5.1 %mid_core.1.refs_5_ = f32[4,1024,1024]{2,1,0:T(8,128)S(1)} custom-call(bf16[128,2048]{1,0:T(8,128)(2,1)S(1)} %collective-permute-done.16.refs_0_, bf16[128,2048]{1,0:T(8,128)(2,1)S(1)} %collective-permute-done.17.refs_1_, bf16[4,1024,2048]{2,1,0:T(8,128)(2,1)S(1)} %get-tuple-element.7.refs_2_.refs_4_, ...), custom_call_target="tpu_custom_call", output_to_operand_aliasing={{}: (3, {})} | custom-call | flops 4294967296 | bytes 16777216 | tf_op jit(solution)/shard_map/mid_core/pallas_call | solution.py:102
  57.0 0.0 copy-start.1
  57.1 5.1 %far.1.products = f32[4,1024,1024]{2,1,0:T(8,128)S(1)} custom-call(bf16[64,2048]{1,0:T(8,128)(2,1)S(1)} %collective-permute-done.10.refs_0_, bf16[64,2048]{1,0:T(8,128)(2,1)S(1)} %collective-permute-done.12.refs_1_, bf16[64,2048]{1,0:T(8,128)(2,1)S(1)} %collective-permute-done.13.refs_2_, ...), custom_call_target="tpu_custom_call", output_to_operand_aliasing={{}: (5, {})} | custom-call | flops 4294967296 | bytes 16777216 | tf_op jit(solution)/shard_map/far/pallas_call | solution.py:102
  62.2 3.4 %collective-permute-done.8.behind = bf16[4,64,1024]{2,1,0:T(8,128)(2,1)S(1)} collective-permute-done((bf16[4,64,1024]{2,1,0:T(8,128)(2,1)S(1)}, bf16[4,64,1024]{2,1,0:T(8,128)(2,1)S(1)}, u32[]{:S(2)}, u32[]{:S(2)}) %collective-permute-start.8) | collective-permute-done | bytes 524320 | tf_op jit(solution)/shard_map/ppermute | solution.py:187
  65.7 2.5 %scores.1 = f32[4,16]{1,0:T(4,128)S(1)} custom-call(s32[16]{0:T(128)S(1)} %copy-done.1, s32[16]{0:T(128)S(1)} %copy-done.2, bf16[4,64,1024]{2,1,0:T(8,128)(2,1)S(1)} %pad_maximum_fusion.own, bf16[4,64,1024]{2,1,0:T(8,128)(2,1)S(1)} %collective-permute-done.3.ahead, bf16[4,64,1024]{2,1,0:T(8,128)(2,1)S(1)} %pad_maximum_fusion.1.far, ...), custom_call_target="tpu_custom_call" | custom-call | flops 1073741824 | bytes 4194304 | tf_op jit(solution)/shard_map/scores/pallas_call | solution.py:149
  68.2 7.7 %all_to_all.10 = f32[8,4,16]{2,1,0:T(4,128)S(1)} all-to-all(f32[8,4,16]{2,1,0:T(4,128)S(1)} %broadcast_in_dim.4), channel_id=1, replica_groups=mesh['row'=8,'col'=16] {'row'}, dimensions={0} | all-to-all | bytes 4096 | tf_op jit(solution)/shard_map/all_to_all | solution.py:163
  75.9 10.2 %all_to_all.11 = f32[16,4,16]{2,1,0:T(4,128)S(1)} all-to-all(f32[16,4,16]{2,1,0:T(4,128)S(1)} %broadcast_in_dim.5), channel_id=1, replica_groups=mesh['row'=8,'col'=16] {'col'}, dimensions={0} | all-to-all | bytes 8192 | tf_op jit(solution)/shard_map/all_to_all | solution.py:163
  86.1 0.6 reduce_sum.19
  (25 shorter events, 0.1 us)
Async XLA Ops:
  0.0 10.4 %collective-permute-start.4 = (bf16[64,1024]{1,0:T(8,128)(2,1)}, bf16[64,1024]{1,0:T(8,128)(2,1)S(1)}, u32[]{:S(2)}, u32[]{:S(2)}) collective-permute-start(bf16[64,1024]{1,0:T(8,128)(2,1)} %param.5), channel_id=1, source_target_pairs={{0,8},{1,9},{2,10},{3,11},{4,12},{5,13},{6,14},{7,15},{8,0},{9,1},... | collective-permute-start | bytes 393224 | tf_op jit(solution)/shard_map/ppermute | solution.py:183
  3.1 29.9 %collective-permute-start.9 = (bf16[128,2048]{1,0:T(8,128)(2,1)}, bf16[128,2048]{1,0:T(8,128)(2,1)S(1)}, u32[]{:S(2)}, u32[]{:S(2)}) collective-permute-start(bf16[128,2048]{1,0:T(8,128)(2,1)} %refs_0_.1), channel_id=1, source_target_pairs={{0,32},{16,48},{32,64},{48,80},{64,96},{80,112},{96,0},{112,16},{1... | collective-permute-start | bytes 1572872 | tf_op jit(solution)/shard_map/ppermute | solution.py:177
  4.7 28.8 %collective-permute-start.11 = (bf16[128,2048]{1,0:T(8,128)(2,1)}, bf16[128,2048]{1,0:T(8,128)(2,1)S(1)}, u32[]{:S(2)}, u32[]{:S(2)}) collective-permute-start(bf16[128,2048]{1,0:T(8,128)(2,1)} %refs_0_.1), channel_id=1, source_target_pairs={{0,96},{16,112},{32,0},{48,16},{64,32},{80,48},{96,64},{112,80},{1... | collective-permute-start | bytes 1572872 | tf_op jit(solution)/shard_map/ppermute | solution.py:178
  6.3 30.1 %collective-permute-start.15 = (bf16[128,2048]{1,0:T(8,128)(2,1)}, bf16[128,2048]{1,0:T(8,128)(2,1)S(1)}, u32[]{:S(2)}, u32[]{:S(2)}) collective-permute-start(bf16[128,2048]{1,0:T(8,128)(2,1)} %refs_0_.1), channel_id=1, source_target_pairs={{0,16},{16,0},{32,48},{48,32},{64,80},{80,64},{96,112},{112,96},{1... | collective-permute-start | bytes 1572872 | tf_op jit(solution)/shard_map/ppermute | solution.py:171
  6.3 10.6 %collective-permute-start = (bf16[64,1024]{1,0:T(8,128)(2,1)}, bf16[64,1024]{1,0:T(8,128)(2,1)S(1)}, u32[]{:S(2)}, u32[]{:S(2)}) collective-permute-start(bf16[64,1024]{1,0:T(8,128)(2,1)} %param.5), channel_id=1, source_target_pairs={{0,3},{1,0},{2,1},{3,2},{4,7},{5,4},{6,5},{7,6},{8,11},{9,8},{10,9... | collective-permute-start | bytes 393224 | tf_op jit(solution)/shard_map/ppermute | solution.py:174
  10.4 7.3 %collective-permute-start.1 = (bf16[64,1024]{1,0:T(8,128)(2,1)}, bf16[64,1024]{1,0:T(8,128)(2,1)S(1)}, u32[]{:S(2)}, u32[]{:S(2)}) collective-permute-start(bf16[64,1024]{1,0:T(8,128)(2,1)} %param.5), channel_id=1, source_target_pairs={{0,2},{1,3},{2,0},{3,1},{4,6},{5,7},{6,4},{7,5},{8,10},{9,11},{10,... | collective-permute-start | bytes 393224 | tf_op jit(solution)/shard_map/ppermute | solution.py:174
  16.9 7.2 %collective-permute-start.2 = (bf16[64,1024]{1,0:T(8,128)(2,1)}, bf16[64,1024]{1,0:T(8,128)(2,1)S(1)}, u32[]{:S(2)}, u32[]{:S(2)}) collective-permute-start(bf16[64,1024]{1,0:T(8,128)(2,1)} %param.5), channel_id=1, source_target_pairs={{0,1},{1,2},{2,3},{3,0},{4,5},{5,6},{6,7},{7,4},{8,9},{9,10},{10,1... | collective-permute-start | bytes 393224 | tf_op jit(solution)/shard_map/ppermute | solution.py:174
  17.7 7.2 %collective-permute-start.5 = (bf16[64,1024]{1,0:T(8,128)(2,1)S(1)}, bf16[64,1024]{1,0:T(8,128)(2,1)S(1)}, u32[]{:S(2)}, u32[]{:S(2)}) collective-permute-start(bf16[64,1024]{1,0:T(8,128)(2,1)S(1)} %collective-permute-done.4), channel_id=1, source_target_pairs={{0,3},{1,0},{2,1},{3,2},{4,7},{5,4},{6,5},{7,6},{8,11},{9,8},{10,9... | collective-permute-start | bytes 393224 | tf_op jit(solution)/shard_map/ppermute | solution.py:174
  24.1 7.6 %collective-permute-start.6 = (bf16[64,1024]{1,0:T(8,128)(2,1)S(1)}, bf16[64,1024]{1,0:T(8,128)(2,1)S(1)}, u32[]{:S(2)}, u32[]{:S(2)}) collective-permute-start(bf16[64,1024]{1,0:T(8,128)(2,1)S(1)} %collective-permute-done.4), channel_id=1, source_target_pairs={{0,2},{1,3},{2,0},{3,1},{4,6},{5,7},{6,4},{7,5},{8,10},{9,11},{10,... | collective-permute-start | bytes 393224 | tf_op jit(solution)/shard_map/ppermute | solution.py:174
  25.0 8.0 %collective-permute-start.7 = (bf16[64,1024]{1,0:T(8,128)(2,1)S(1)}, bf16[64,1024]{1,0:T(8,128)(2,1)S(1)}, u32[]{:S(2)}, u32[]{:S(2)}) collective-permute-start(bf16[64,1024]{1,0:T(8,128)(2,1)S(1)} %collective-permute-done.4), channel_id=1, source_target_pairs={{0,1},{1,2},{2,3},{3,0},{4,5},{5,6},{6,7},{7,4},{8,9},{9,10},{10,1... | collective-permute-start | bytes 393224 | tf_op jit(solution)/shard_map/ppermute | solution.py:174
  31.7 30.5 %collective-permute-start.3 = (bf16[4,64,1024]{2,1,0:T(8,128)(2,1)S(1)}, bf16[4,64,1024]{2,1,0:T(8,128)(2,1)S(1)}, u32[]{:S(2)}, u32[]{:S(2)}) collective-permute-start(bf16[4,64,1024]{2,1,0:T(8,128)(2,1)S(1)} %pad_maximum_fusion.own), channel_id=1, source_target_pairs={{0,12},{1,13},{2,14},{3,15},{4,0},{5,1},{6,2},{7,3},{8,4},{9,5},{1... | collective-permute-start | bytes 1572872 | tf_op jit(solution)/shard_map/ppermute | solution.py:186
  33.1 17.5 %collective-permute-start.10 = (bf16[64,2048]{1,0:T(8,128)(2,1)S(1)}, bf16[64,2048]{1,0:T(8,128)(2,1)S(1)}, u32[]{:S(2)}, u32[]{:S(2)}) collective-permute-start(bf16[64,2048]{1,0:T(8,128)(2,1)S(1)} %slice.8), channel_id=1, source_target_pairs={{0,32},{16,48},{32,64},{48,80},{64,96},{80,112},{96,0},{112,16},{1... | collective-permute-start | bytes 786440 | tf_op jit(solution)/shard_map/ppermute | solution.py:189
  33.5 17.9 %collective-permute-start.12 = (bf16[64,2048]{1,0:T(8,128)(2,1)S(1)}, bf16[64,2048]{1,0:T(8,128)(2,1)S(1)}, u32[]{:S(2)}, u32[]{:S(2)}) collective-permute-start(bf16[64,2048]{1,0:T(8,128)(2,1)S(1)} %slice.9), channel_id=1, source_target_pairs={{0,96},{16,112},{32,0},{48,16},{64,32},{80,48},{96,64},{112,80},{1... | collective-permute-start | bytes 786440 | tf_op jit(solution)/shard_map/ppermute | solution.py:190
  36.5 14.9 %collective-permute-start.16 = (bf16[128,2048]{1,0:T(8,128)(2,1)S(1)}, bf16[128,2048]{1,0:T(8,128)(2,1)S(1)}, u32[]{:S(2)}, u32[]{:S(2)}) collective-permute-start(bf16[128,2048]{1,0:T(8,128)(2,1)S(1)} %collective-permute-done.9.refs_0_), channel_id=1, source_target_pairs={{0,16},{16,0},{32,48},{48,32},{64,80},{80,64},{96,112},{112,96},{1... | collective-permute-start | bytes 1572872 | tf_op jit(solution)/shard_map/ppermute | solution.py:171
  36.5 15.4 %collective-permute-start.17 = (bf16[128,2048]{1,0:T(8,128)(2,1)S(1)}, bf16[128,2048]{1,0:T(8,128)(2,1)S(1)}, u32[]{:S(2)}, u32[]{:S(2)}) collective-permute-start(bf16[128,2048]{1,0:T(8,128)(2,1)S(1)} %collective-permute-done.11.refs_1_), channel_id=1, source_target_pairs={{0,16},{16,0},{32,48},{48,32},{64,80},{80,64},{96,112},{112,96},{1... | collective-permute-start | bytes 1572872 | tf_op jit(solution)/shard_map/ppermute | solution.py:171
  37.0 1.0 %copy-start = (bf16[128,2048]{1,0:T(8,128)(2,1)S(1)}, bf16[128,2048]{1,0:T(8,128)(2,1)}, u32[]{:S(2)}) copy-start(bf16[128,2048]{1,0:T(8,128)(2,1)} %refs_0_.1) | copy-start | bytes 1572868
  50.5 15.1 %collective-permute-start.8 = (bf16[4,64,1024]{2,1,0:T(8,128)(2,1)S(1)}, bf16[4,64,1024]{2,1,0:T(8,128)(2,1)S(1)}, u32[]{:S(2)}, u32[]{:S(2)}) collective-permute-start(bf16[4,64,1024]{2,1,0:T(8,128)(2,1)S(1)} %pad_maximum_fusion.own), channel_id=1, source_target_pairs={{0,4},{1,5},{2,6},{3,7},{4,8},{5,9},{6,10},{7,11},{8,12},{9,13},{1... | collective-permute-start | bytes 1572872 | tf_op jit(solution)/shard_map/ppermute | solution.py:187
  51.4 5.7 %collective-permute-start.13 = (bf16[64,2048]{1,0:T(8,128)(2,1)S(1)}, bf16[64,2048]{1,0:T(8,128)(2,1)S(1)}, u32[]{:S(2)}, u32[]{:S(2)}) collective-permute-start(bf16[64,2048]{1,0:T(8,128)(2,1)S(1)} %collective-permute-done.10.refs_0_), channel_id=1, source_target_pairs={{0,16},{16,0},{32,48},{48,32},{64,80},{80,64},{96,112},{112,96},{1... | collective-permute-start | bytes 786440 | tf_op jit(solution)/shard_map/ppermute | solution.py:171
  51.4 5.7 %collective-permute-start.14 = (bf16[64,2048]{1,0:T(8,128)(2,1)S(1)}, bf16[64,2048]{1,0:T(8,128)(2,1)S(1)}, u32[]{:S(2)}, u32[]{:S(2)}) collective-permute-start(bf16[64,2048]{1,0:T(8,128)(2,1)S(1)} %collective-permute-done.12.refs_1_), channel_id=1, source_target_pairs={{0,16},{16,0},{32,48},{48,32},{64,80},{80,64},{96,112},{112,96},{1... | collective-permute-start | bytes 786440 | tf_op jit(solution)/shard_map/ppermute | solution.py:171
  57.0 8.6 %copy-start.1 = (s32[16]{0:T(128)S(1)}, s32[16]{0:T(128)}, u32[]{:S(2)}) copy-start(s32[16]{0:T(128)} %seq_start.1) | copy-start | bytes 196
  57.0 8.6 %copy-start.2 = (s32[16]{0:T(128)S(1)}, s32[16]{0:T(128)}, u32[]{:S(2)}) copy-start(s32[16]{0:T(128)} %seq_len.1) | copy-start | bytes 196

commit v2 on v0

v2 whole, which is shorter than its diff:
```python
import functools

import jax
import jax.numpy as jnp
from jax import lax
from jax.experimental import pallas as pl
from jax.experimental.pallas import tpu as pltpu
from jax.sharding import PartitionSpec as P

NT = (((1,), (1,)), ((), ()))
SLOT = 64
BLOCK = 128
VMEM = pl.BlockSpec(memory_space=pltpu.VMEM)
SMEM = pl.BlockSpec(memory_space=pltpu.SMEM)
HBM = pl.BlockSpec(memory_space=pltpu.HBM)
TOKEN = pltpu.VMEM((8, 128), jnp.float32)
SMALL = pltpu.CompilerParams(vmem_limit_bytes=8 << 20)
WEIGHT = 10


def along_y(shift):
    return [(i, ((i // 2 + shift) % 4) * 2 + i % 2) for i in range(8)]


def along_z(col, shift):
    return col // 4 * 4 + (col + shift) % 4


def along_x(col, shift):
    return (col + 4 * shift) % 16


def along_both(first, second, shift):
    return [
        (16 * row + col, 16 * row + (first, second)[row % 2](col, shift)) for row in range(8) for col in range(16)
    ]


OTHER_CORE = [(i, i ^ 1) for i in range(8)]
Y_BY_CORE = [(i, (i + 2 - 4 * (i % 2)) % 8) for i in range(8)]


def resident(value):
    return pltpu.with_memory_space_constraint(value, pltpu.VMEM)


def my_core():
    return lax.axis_index("row") % 2


def first_row(dy, dcore):
    index = lax.axis_index("row")
    y, core = index // 2, index % 2
    return pl.multiple_of((y + dy) % 4 * 2 * BLOCK + (core + dcore) % 2 * BLOCK, BLOCK)


def store_products(result, products, places, q, columns=slice(None)):
    for i, (dy, dcore) in enumerate(places):
        products[q, pl.ds(first_row(dy, dcore), BLOCK), columns] = result[i * BLOCK : (i + 1) * BLOCK]


def near_kernel(places, own, other, queries, products, held, token, rows, sems):
    nq, width, _ = held.shape
    half = width // 2
    chunks = [(0, slice(0, half)), (0, slice(half, width))]
    chunks += [(q, slice(0, width)) for q in range(1, nq - 1)]
    chunks += [(nq - 1, slice(0, half)), (nq - 1, slice(half, width))]
    copies = [
        pltpu.make_async_copy(queries.at[q, part], held.at[q, part], sems.at[i]) for i, (q, part) in enumerate(chunks)
    ]
    block_copies = [
        pltpu.make_async_copy(block, rows.at[pl.ds(i * BLOCK, BLOCK)], sems.at[len(copies) + i])
        for i, block in enumerate((own, other))
    ]
    for copy in block_copies + copies:
        copy.start()
    token[...] = jnp.zeros_like(token)
    for copy in block_copies:
        copy.wait()
    for copy, (q, part) in zip(copies, chunks, strict=True):
        copy.wait()
        result = lax.dot_general(rows[...], held[q, part], NT, preferred_element_type=jnp.float32)
        store_products(result, products, places, q, part)


def near_products(places, own, other, queries, tokens):
    nq, width, depth = queries.shape
    return pl.pallas_call(
        functools.partial(near_kernel, places),
        in_specs=[HBM, VMEM, HBM],
        out_specs=[VMEM] * 3,
        out_shape=[pltpu.VMEM((nq, tokens, width), jnp.float32), pltpu.VMEM(queries.shape, queries.dtype), TOKEN],
        scratch_shapes=[pltpu.VMEM((2 * BLOCK, depth), own.dtype), pltpu.SemaphoreType.DMA((2 * nq + 2,))],
        compiler_params=SMALL,
        cost_estimate=pl.CostEstimate(
            flops=WEIGHT * 4 * BLOCK * queries.size, bytes_accessed=2 * queries.size, transcendentals=0
        ),
        name="near",
    )(pltpu.with_memory_space_constraint(own, pltpu.HBM), other, queries)


def next_kernel(places, computed, rows, held, _, products, token):
    token[...] = jnp.zeros_like(token)
    for q in range(*computed):
        result = lax.dot_general(rows[...], held[q], NT, preferred_element_type=jnp.float32)
        store_products(result, products, places, q)


def next_products(name, places, rows, held, products, computed):
    share = computed[1] - computed[0]
    return pl.pallas_call(
        functools.partial(next_kernel, places, computed),
        in_specs=[VMEM] * 3,
        out_specs=[VMEM] * 2,
        out_shape=[pltpu.VMEM(products.shape, products.dtype), TOKEN],
        input_output_aliases={2: 0},
        compiler_params=SMALL,
        cost_estimate=pl.CostEstimate(
            flops=WEIGHT * share * rows.shape[0] * held.size // 2, bytes_accessed=2 * rows.size, transcendentals=0
        ),
        name=name,
    )(rows, resident(held), resident(products))


def pair_kernel(below, above, _, pair, onward):
    pair[:BLOCK, :] = below[...]
    pair[BLOCK:, :] = above[...]

    @pl.when(my_core() == 0)
    def _():
        onward[...] = below[...]

    @pl.when(my_core() == 1)
    def _():
        onward[...] = above[...]


def pair_up(below, above, token):
    rows, depth = below.shape
    return pl.pallas_call(
        pair_kernel,
        in_specs=[VMEM] * 3,
        out_specs=[VMEM] * 2,
        out_shape=[pltpu.VMEM((2 * rows, depth), below.dtype), pltpu.VMEM(below.shape, below.dtype)],
        compiler_params=SMALL,
        name="pair",
    )(below, above, token)


def stack_kernel(*refs):
    *blocks, _, out = refs
    for i, block in enumerate(blocks):
        out[i] = block[...]


def stack(blocks, token):
    return pl.pallas_call(
        stack_kernel,
        in_specs=[VMEM] * (len(blocks) + 1),
        out_specs=VMEM,
        out_shape=pltpu.VMEM((len(blocks),) + blocks[0].shape, blocks[0].dtype),
        compiler_params=SMALL,
        name="stack",
    )(*blocks, token)


def join_kernel(first, second, both):
    both[:BLOCK, :] = first[...]
    both[BLOCK:, :] = second[...]


def join(first, second):
    rows, depth = first.shape
    return pl.pallas_call(
        join_kernel,
        in_specs=[VMEM] * 2,
        out_specs=VMEM,
        out_shape=pltpu.VMEM((2 * rows, depth), first.dtype),
        compiler_params=SMALL,
        name="join",
    )(first, second)


def score_kernel(seq_start, seq_len, own, ahead, far, behind, products, out, lanes):
    col = lax.axis_index("col")
    x, z, core = col // 4, col % 4, my_core()
    nq = out.shape[0]
    width = products.shape[2]
    position = lax.broadcasted_iota(jnp.int32, (SLOT, 128), 0)
    for d, block in enumerate((own, ahead, far, behind)):

        def one_slot(i, carry, d=d, block=block):
            dx, dz = jnp.where(core == 0, d, i), jnp.where(core == 0, i, d)
            slot = (x + dx) % 4 * 4 + (z + dz) % 4
            base = pl.multiple_of(slot * SLOT, SLOT)
            token = position + base
            start = seq_start[slot]
            inside = (token >= start) & (token < start + seq_len[slot])
            totals = [jnp.zeros((SLOT, 128), jnp.float32) for _ in range(nq)]
            for w in range(0, width, 128):
                act = block[i, :, w : w + 128].astype(jnp.float32)
                for q in range(nq):
                    totals[q] += products[q, pl.ds(base, SLOT), w : w + 128] * act
            for q in range(nq):
                kept = jnp.where(inside, totals[q], 0.0)
                lanes[q, pl.ds(slot, 1), :] = jnp.sum(kept, axis=0, keepdims=True)
            return carry

        lax.fori_loop(0, 4, one_slot, 0)
    ones = jnp.ones((8, 128), jnp.float32)
    for q in range(nq):
        sums = lax.dot_general(ones, lanes[q], NT, precision=lax.Precision.HIGHEST, preferred_element_type=jnp.float32)
        out[q : q + 1, :] = sums[:1, :]


def partial_scores(seq_start, seq_len, acts, products):
    nq = products.shape[0]
    nseq = seq_start.shape[0]
    return pl.pallas_call(
        score_kernel,
        in_specs=[SMEM] * 2 + [VMEM] * (len(acts) + 1),
        out_specs=VMEM,
        out_shape=jax.ShapeDtypeStruct((nq, nseq), jnp.float32),
        scratch_shapes=[pltpu.VMEM((nq, nseq, 128), jnp.float32)],
        compiler_params=SMALL,
        cost_estimate=pl.CostEstimate(flops=1 << 30, bytes_accessed=4 << 20, transcendentals=0),
        name="scores",
    )(seq_start, seq_len, *acts, resident(products))


def from_all(value, axis):
    copies = jnp.broadcast_to(value[None], (lax.axis_size(axis),) + value.shape)
    return lax.all_to_all(copies, axis, 0, 0, tiled=True)


def on_device(activations, out_grads, queries, seq_start, seq_len):
    tokens = SLOT * seq_start.shape[0]
    nq = queries.shape[0]

    def to_core(block):
        return lax.ppermute(block, "row", OTHER_CORE)

    below = lax.ppermute(out_grads, "row", along_y(1))
    above = lax.ppermute(out_grads, "row", along_y(-1))
    other = to_core(out_grads)
    first_acts = [lax.ppermute(activations, ("row", "col"), along_both(along_z, along_x, -d)) for d in (1, 2, 3)]

    products, held, token = near_products([(0, 0), (0, 1)], out_grads, other, queries, tokens)
    own_act = stack([activations] + first_acts, token)
    acts = [own_act] + [lax.ppermute(own_act, ("row", "col"), along_both(along_x, along_z, -d)) for d in (1, 2, 3)]
    pair, onward = pair_up(below, above, token)
    pair_other = to_core(pair)
    far = lax.ppermute(onward, "row", Y_BY_CORE)

    products, token = next_products("mid", [(3, 0), (1, 0)], pair, held, products, (0, nq))
    places = [(3, 1), (1, 1)]
    products, token = next_products("other_low", places, pair_other, held, products, (0, nq // 2))
    (far,) = stack([far], token)
    far_other = to_core(far)
    products, token = next_products("other_high", places, pair_other, held, products, (nq // 2, nq))
    products, token = next_products("far", [(2, 0), (2, 1)], join(far, far_other), held, products, (0, nq))
    scores = partial_scores(seq_start, seq_len, acts, products)
    scores = jnp.sum(from_all(scores, "row"), axis=0)
    return jnp.sum(from_all(scores, "col"), axis=0)


def solution(mesh):
    in_specs = (P("col", "row"), P("row", "col"), P(None, "row", "col"), P(), P())
    return jax.shard_map(on_device, mesh=mesh, in_specs=in_specs, out_specs=P(), check_vma=False)
```

time: 187 us -> 64.4 us (0.34)
  waiting for transfers between devices: 76.9 us -> 2.7 us
  blocking collectives: 64.4 us -> 20.6 us
  Pallas kernels: 0 us -> 25.9 us
  matrix products: 23.5 us -> 0 us
  starting transfers between devices: 0.04 us -> 14.2 us
  between operations: 13.4 us -> 0.14 us
  local copies, waits for them, and re-layouts: 6.88 us -> 0.03 us
    all_gather x2 -> x0, waiting for transfers between devices: 75.5 us -> none  [the longest x1 40.5 us: on_device(): act_all = lax.all_gather(activations, 'col', axis=0, tiled=True)]
    psum x1 -> x0, blocking collectives: 64.4 us -> none  [on_device(): return lax.psum(partial_value, ('row', 'col'))]
    pallas_call x0 -> x10, Pallas kernels: none -> 25.9 us  [the longest x4 15.1 us: next_products(): pl.pallas_call(functools.partial(next_kernel, places, computed), in_specs...]
    dot_general x2 -> x0, matrix products: 23.5 us -> none  [the longest x1 23.2 us: token_scores(): jnp.einsum('ti,qij->qtj', act_block, queries, preferred_element_type=jnp....]
    all_to_all x0 -> x2, blocking collectives: none -> 20.6 us  [from_all(): return lax.all_to_all(copies, axis, 0, 0, tiled=True)]
    ppermute x0 -> x12, starting transfers between devices: none -> 14.2 us  [the longest x3 5.42 us: on_device(): lax.ppermute(activations, ('row', 'col'), along_both(along_z, along_x, -d))]
    convert_element_type x1 -> x0, local copies, waits for them, and re-layouts: 6.87 us -> none  [token_scores(): return jnp.sum(products * grad_block.astype(jnp.float32)[None], axis=2)]
    ppermute x0 -> x12, waiting for transfers between devices: none -> 2.7 us  [the longest x1 2.68 us: on_device(): far = lax.ppermute(onward, 'row', Y_BY_CORE)]
  transfers between devices with their start and end apart: 2 -> 12, of which waited for: 2 -> 1; matrix products, arithmetic and copies ran while one was open for 4% -> 0% of each run, Pallas kernels for 0% -> 36%
where the time goes in v2:
time: 64.4 us; the launch traced here: 64.2 us
  Pallas kernels  25.9 us (40%)
  blocking collectives  20.6 us (32%)
  starting transfers between devices  14.2 us (22%)
  waiting for transfers between devices  2.7 us (4%)
    all_to_all x2, blocking collectives, from_all(): return lax.all_to_all(copies, axis, 0, 0, tiled=True)  20.6 us
    pallas_call x4, Pallas kernels, next_products(): pl.pallas_call(functools.partial(next_kernel, places, computed), in_specs...  15.1 us
    pallas_call x1, Pallas kernels, near_products(): pl.pallas_call(functools.partial(near_kernel, places), in_specs=[HBM, VME...  7.78 us
    ppermute x3, starting transfers between devices, on_device(): lax.ppermute(activations, ('row', 'col'), along_both(along_z, along_x, -d))  5.42 us
    ppermute x3, starting transfers between devices, on_device(): lax.ppermute(own_act, ('row', 'col'), along_both(along_x, along_z, -d))  4.51 us
    pallas_call x1, Pallas kernels, partial_scores(): pl.pallas_call(score_kernel, in_specs=[SMEM] * 2 + [VMEM] * (len(acts) +...  2.84 us
    ppermute x1, waiting for transfers between devices, on_device(): far = lax.ppermute(onward, 'row', Y_BY_CORE)  2.68 us
    ppermute x1, starting transfers between devices, on_device(): below = lax.ppermute(out_grads, 'row', along_y(1))  1.72 us
  transfers between devices with their start and end apart: 12, of which 1 were waited for; matrix products, arithmetic and copies ran while one was open for 0% of the time, Pallas kernels for 36%

profile of v2, /device:TPU:0, one launch (start us, length us, event | category | flops | bytes accessed | tf_op | source)
XLA Modules:
  0.0 64.2 jit_solution(9986779351033160908)
XLA Ops:
  0.0 0.0 collective-permute-start.3
  0.0 1.7 %collective-permute-start.7 = (bf16[128,2048]{1,0:T(8,128)(2,1)}, bf16[128,2048]{1,0:T(8,128)(2,1)S(1)}, u32[]{:S(2)}, u32[]{:S(2)}) collective-permute-start(bf16[128,2048]{1,0:T(8,128)(2,1)} %own.1), channel_id=1, source_target_pairs={{0,32},{16,48},{32,64},{48,80},{64,96},{80,112},{96,0},{112,16},{1... | collective-permute-start | bytes 1572872 | tf_op jit(solution)/shard_map/ppermute | solution.py:243
  1.7 1.5 %collective-permute-start.8 = (bf16[128,2048]{1,0:T(8,128)(2,1)}, bf16[128,2048]{1,0:T(8,128)(2,1)S(1)}, u32[]{:S(2)}, u32[]{:S(2)}) collective-permute-start(bf16[128,2048]{1,0:T(8,128)(2,1)} %own.1), channel_id=1, source_target_pairs={{0,96},{16,112},{32,0},{48,16},{64,32},{80,48},{96,64},{112,80},{1... | collective-permute-start | bytes 1572872 | tf_op jit(solution)/shard_map/ppermute | solution.py:244
  3.3 4.2 %collective-permute-start = (bf16[64,1024]{1,0:T(8,128)(2,1)}, bf16[64,1024]{1,0:T(8,128)(2,1)S(1)}, u32[]{:S(2)}, u32[]{:S(2)}) collective-permute-start(bf16[64,1024]{1,0:T(8,128)(2,1)} %refs_0_.1), channel_id=1, source_target_pairs={{0,3},{1,0},{2,1},{3,2},{4,7},{5,4},{6,5},{7,6},{8,11},{9,8},{10,9... | collective-permute-start | bytes 393224 | tf_op jit(solution)/shard_map/ppermute | solution.py:246
  7.4 0.0 collective-permute-start.1
  7.4 0.0 collective-permute-done.3.other
  7.4 1.3 %collective-permute-start.2 = (bf16[64,1024]{1,0:T(8,128)(2,1)}, bf16[64,1024]{1,0:T(8,128)(2,1)S(1)}, u32[]{:S(2)}, u32[]{:S(2)}) collective-permute-start(bf16[64,1024]{1,0:T(8,128)(2,1)} %refs_0_.1), channel_id=1, source_target_pairs={{0,1},{1,2},{2,3},{3,0},{4,5},{5,6},{6,7},{7,4},{8,9},{9,10},{10,1... | collective-permute-start | bytes 393224 | tf_op jit(solution)/shard_map/ppermute | solution.py:246
  8.7 7.8 %near.1 = (f32[4,1024,1024]{2,1,0:T(8,128)S(1)}, bf16[4,1024,2048]{2,1,0:T(8,128)(2,1)S(1)}, f32[8,128]{1,0:T(8,128)S(1)}) custom-call(bf16[128,2048]{1,0:T(8,128)(2,1)} %own.1, bf16[128,2048]{1,0:T(8,128)(2,1)S(1)} %collective-permute-done.3.other, bf16[4,1024,2048]{2,1,0:T(8,128)(2,1)} %queries.1), custom_call_target="tpu_custom_call" | custom-call | flops 42949672960 | bytes 16777216 | tf_op jit(solution)/shard_map/near/pallas_call | solution.py:88
  16.5 0.0 collective-permute-done.refs_1_
  16.5 0.0 collective-permute-done.1.refs_2_
  16.6 2.8 %collective-permute-start.4 = (bf16[4,64,1024]{2,1,0:T(8,128)(2,1)S(1)}, bf16[4,64,1024]{2,1,0:T(8,128)(2,1)S(1)}, u32[]{:S(2)}, u32[]{:S(2)}) collective-permute-start(bf16[4,64,1024]{2,1,0:T(8,128)(2,1)S(1)} %stack.2.own), channel_id=1, source_target_pairs={{0,12},{1,13},{2,14},{3,15},{4,0},{5,1},{6,2},{7,3},{8,4},{9,5},{1... | collective-permute-start | bytes 1572872 | tf_op jit(solution)/shard_map/ppermute | solution.py:250
  19.4 0.8 %collective-permute-start.5 = (bf16[4,64,1024]{2,1,0:T(8,128)(2,1)S(1)}, bf16[4,64,1024]{2,1,0:T(8,128)(2,1)S(1)}, u32[]{:S(2)}, u32[]{:S(2)}) collective-permute-start(bf16[4,64,1024]{2,1,0:T(8,128)(2,1)S(1)} %stack.2.own), channel_id=1, source_target_pairs={{0,8},{1,9},{2,10},{3,11},{4,12},{5,13},{6,14},{7,15},{8,0},{9,1},... | collective-permute-start | bytes 1572872 | tf_op jit(solution)/shard_map/ppermute | solution.py:250
  20.2 0.9 %collective-permute-start.6 = (bf16[4,64,1024]{2,1,0:T(8,128)(2,1)S(1)}, bf16[4,64,1024]{2,1,0:T(8,128)(2,1)S(1)}, u32[]{:S(2)}, u32[]{:S(2)}) collective-permute-start(bf16[4,64,1024]{2,1,0:T(8,128)(2,1)S(1)} %stack.2.own), channel_id=1, source_target_pairs={{0,4},{1,5},{2,6},{3,7},{4,8},{5,9},{6,10},{7,11},{8,12},{9,13},{1... | collective-permute-start | bytes 1572872 | tf_op jit(solution)/shard_map/ppermute | solution.py:250
  21.1 0.0 collective-permute-done.7.below
  21.1 0.0 collective-permute-done.8.above
  21.1 0.1 pair.1
  21.2 0.1 collective-permute-start.10
  21.3 0.6 collective-permute-start.9
  21.9 5.0 %mid.1 = (f32[4,1024,1024]{2,1,0:T(8,128)S(1)}, f32[8,128]{1,0:T(8,128)}) custom-call(bf16[256,2048]{1,0:T(8,128)(2,1)S(1)} %get-tuple-element.17.rows, bf16[4,1024,2048]{2,1,0:T(8,128)(2,1)S(1)} %get-tuple-element.18.held, f32[4,1024,1024]{2,1,0:T(8,128)S(1)} %get-tuple-element.19._), custom_call_target="tpu_custom_call", output_to_operand_aliasing={{0}: (2, {})} | custom-call | flops 42949672960 | bytes 1048576 | tf_op jit(solution)/shard_map/mid/pallas_call | solution.py:111
  26.9 2.4 %other_low.1 = (f32[4,1024,1024]{2,1,0:T(8,128)S(1)}, f32[8,128]{1,0:T(8,128)S(1)}) custom-call(bf16[256,2048]{1,0:T(8,128)(2,1)S(1)} %collective-permute-done.10.rows, bf16[4,1024,2048]{2,1,0:T(8,128)(2,1)S(1)} %get-tuple-element.18.held, f32[4,1024,1024]{2,1,0:T(8,128)S(1)} %get-tuple-element.20._), custom_call_target="tpu_custom_call", output_to_operand_aliasing={{0}: (2, {})} | custom-call | flops 21474836480 | bytes 1048576 | tf_op jit(solution)/shard_map/other_low/pallas_call | solution.py:111
  29.3 2.7 %collective-permute-done.9.refs_0_ = bf16[128,2048]{1,0:T(8,128)(2,1)S(1)} collective-permute-done((bf16[128,2048]{1,0:T(8,128)(2,1)S(1)}, bf16[128,2048]{1,0:T(8,128)(2,1)S(1)}, u32[]{:S(2)}, u32[]{:S(2)}) %collective-permute-start.9) | collective-permute-done | bytes 524320 | tf_op jit(solution)/shard_map/ppermute | solution.py:253
  32.0 0.3 collective-permute-start.11
  32.3 2.8 %other_high.1 = (f32[4,1024,1024]{2,1,0:T(8,128)S(1)}, f32[8,128]{1,0:T(8,128)}) custom-call(bf16[256,2048]{1,0:T(8,128)(2,1)S(1)} %collective-permute-done.10.rows, bf16[4,1024,2048]{2,1,0:T(8,128)(2,1)S(1)} %get-tuple-element.18.held, f32[4,1024,1024]{2,1,0:T(8,128)S(1)} %get-tuple-element.22._), custom_call_target="tpu_custom_call", output_to_operand_aliasing={{0}: (2, {})} | custom-call | flops 21474836480 | bytes 1048576 | tf_op jit(solution)/shard_map/other_high/pallas_call | solution.py:111
  35.0 0.1 join.1.rows
  35.1 0.0 copy-start.1
  35.1 0.0 copy-start.2
  35.1 5.0 %far.1 = (f32[4,1024,1024]{2,1,0:T(8,128)S(1)}, f32[8,128]{1,0:T(8,128)}) custom-call(bf16[256,2048]{1,0:T(8,128)(2,1)S(1)} %join.1.rows, bf16[4,1024,2048]{2,1,0:T(8,128)(2,1)S(1)} %get-tuple-element.18.held, f32[4,1024,1024]{2,1,0:T(8,128)S(1)} %get-tuple-element.23._), custom_call_target="tpu_custom_call", output_to_operand_aliasing={{0}: (2, {})} | custom-call | flops 42949672960 | bytes 1048576 | tf_op jit(solution)/shard_map/far/pallas_call | solution.py:111
  40.1 0.0 collective-permute-done.6.behind
  40.1 2.8 %scores.1 = f32[4,16]{1,0:T(4,128)S(1)} custom-call(s32[16]{0:T(128)S(1)} %copy-done.1, s32[16]{0:T(128)S(1)} %copy-done.2, bf16[4,64,1024]{2,1,0:T(8,128)(2,1)S(1)} %stack.2.own, bf16[4,64,1024]{2,1,0:T(8,128)(2,1)S(1)} %collective-permute-done.4.ahead, bf16[4,64,1024]{2,1,0:T(8,128)(2,1)S(1)} %collective-permute-done.5.far, ...), custom_call_target="tpu_custom_call" | custom-call | flops 1073741824 | bytes 4194304 | tf_op jit(solution)/shard_map/scores/pallas_call | solution.py:219
  43.0 7.7 %all_to_all.10 = f32[8,4,16]{2,1,0:T(4,128)S(1)} all-to-all(f32[8,4,16]{2,1,0:T(4,128)S(1)} %broadcast_in_dim.4), channel_id=1, replica_groups=mesh['row'=8,'col'=16] {'row'}, dimensions={0} | all-to-all | bytes 4096 | tf_op jit(solution)/shard_map/all_to_all | solution.py:233
  50.7 12.9 %all_to_all.11 = f32[16,4,16]{2,1,0:T(4,128)S(1)} all-to-all(f32[16,4,16]{2,1,0:T(4,128)S(1)} %broadcast_in_dim.5), channel_id=1, replica_groups=mesh['row'=8,'col'=16] {'col'}, dimensions={0} | all-to-all | bytes 8192 | tf_op jit(solution)/shard_map/all_to_all | solution.py:233
  63.6 0.6 reduce_sum.19
  (14 shorter events, 0.1 us)
Async XLA Ops:
  0.0 16.5 %copy-start = (bf16[64,1024]{1,0:T(8,128)(2,1)S(1)}, bf16[64,1024]{1,0:T(8,128)(2,1)}, u32[]{:S(2)}) copy-start(bf16[64,1024]{1,0:T(8,128)(2,1)} %refs_0_.1) | copy-start | bytes 393220
  0.0 7.4 %collective-permute-start.3 = (bf16[128,2048]{1,0:T(8,128)(2,1)}, bf16[128,2048]{1,0:T(8,128)(2,1)S(1)}, u32[]{:S(2)}, u32[]{:S(2)}) collective-permute-start(bf16[128,2048]{1,0:T(8,128)(2,1)} %own.1), channel_id=1, source_target_pairs={{0,16},{16,0},{32,48},{48,32},{64,80},{80,64},{96,112},{112,96},{1... | collective-permute-start | bytes 1572872 | tf_op jit(solution)/shard_map/ppermute | solution.py:241
  0.0 21.1 %collective-permute-start.7 = (bf16[128,2048]{1,0:T(8,128)(2,1)}, bf16[128,2048]{1,0:T(8,128)(2,1)S(1)}, u32[]{:S(2)}, u32[]{:S(2)}) collective-permute-start(bf16[128,2048]{1,0:T(8,128)(2,1)} %own.1), channel_id=1, source_target_pairs={{0,32},{16,48},{32,64},{48,80},{64,96},{80,112},{96,0},{112,16},{1... | collective-permute-start | bytes 1572872 | tf_op jit(solution)/shard_map/ppermute | solution.py:243
  1.7 19.4 %collective-permute-start.8 = (bf16[128,2048]{1,0:T(8,128)(2,1)}, bf16[128,2048]{1,0:T(8,128)(2,1)S(1)}, u32[]{:S(2)}, u32[]{:S(2)}) collective-permute-start(bf16[128,2048]{1,0:T(8,128)(2,1)} %own.1), channel_id=1, source_target_pairs={{0,96},{16,112},{32,0},{48,16},{64,32},{80,48},{96,64},{112,80},{1... | collective-permute-start | bytes 1572872 | tf_op jit(solution)/shard_map/ppermute | solution.py:244
  3.3 13.2 %collective-permute-start = (bf16[64,1024]{1,0:T(8,128)(2,1)}, bf16[64,1024]{1,0:T(8,128)(2,1)S(1)}, u32[]{:S(2)}, u32[]{:S(2)}) collective-permute-start(bf16[64,1024]{1,0:T(8,128)(2,1)} %refs_0_.1), channel_id=1, source_target_pairs={{0,3},{1,0},{2,1},{3,2},{4,7},{5,4},{6,5},{7,6},{8,11},{9,8},{10,9... | collective-permute-start | bytes 393224 | tf_op jit(solution)/shard_map/ppermute | solution.py:246
  7.4 9.1 %collective-permute-start.1 = (bf16[64,1024]{1,0:T(8,128)(2,1)}, bf16[64,1024]{1,0:T(8,128)(2,1)S(1)}, u32[]{:S(2)}, u32[]{:S(2)}) collective-permute-start(bf16[64,1024]{1,0:T(8,128)(2,1)} %refs_0_.1), channel_id=1, source_target_pairs={{0,2},{1,3},{2,0},{3,1},{4,6},{5,7},{6,4},{7,5},{8,10},{9,11},{10,... | collective-permute-start | bytes 393224 | tf_op jit(solution)/shard_map/ppermute | solution.py:246
  7.4 9.1 %collective-permute-start.2 = (bf16[64,1024]{1,0:T(8,128)(2,1)}, bf16[64,1024]{1,0:T(8,128)(2,1)S(1)}, u32[]{:S(2)}, u32[]{:S(2)}) collective-permute-start(bf16[64,1024]{1,0:T(8,128)(2,1)} %refs_0_.1), channel_id=1, source_target_pairs={{0,1},{1,2},{2,3},{3,0},{4,5},{5,6},{6,7},{7,4},{8,9},{9,10},{10,1... | collective-permute-start | bytes 393224 | tf_op jit(solution)/shard_map/ppermute | solution.py:246
  16.6 23.5 %collective-permute-start.4 = (bf16[4,64,1024]{2,1,0:T(8,128)(2,1)S(1)}, bf16[4,64,1024]{2,1,0:T(8,128)(2,1)S(1)}, u32[]{:S(2)}, u32[]{:S(2)}) collective-permute-start(bf16[4,64,1024]{2,1,0:T(8,128)(2,1)S(1)} %stack.2.own), channel_id=1, source_target_pairs={{0,12},{1,13},{2,14},{3,15},{4,0},{5,1},{6,2},{7,3},{8,4},{9,5},{1... | collective-permute-start | bytes 1572872 | tf_op jit(solution)/shard_map/ppermute | solution.py:250
  19.4 20.7 %collective-permute-start.5 = (bf16[4,64,1024]{2,1,0:T(8,128)(2,1)S(1)}, bf16[4,64,1024]{2,1,0:T(8,128)(2,1)S(1)}, u32[]{:S(2)}, u32[]{:S(2)}) collective-permute-start(bf16[4,64,1024]{2,1,0:T(8,128)(2,1)S(1)} %stack.2.own), channel_id=1, source_target_pairs={{0,8},{1,9},{2,10},{3,11},{4,12},{5,13},{6,14},{7,15},{8,0},{9,1},... | collective-permute-start | bytes 1572872 | tf_op jit(solution)/shard_map/ppermute | solution.py:250
  20.2 19.9 %collective-permute-start.6 = (bf16[4,64,1024]{2,1,0:T(8,128)(2,1)S(1)}, bf16[4,64,1024]{2,1,0:T(8,128)(2,1)S(1)}, u32[]{:S(2)}, u32[]{:S(2)}) collective-permute-start(bf16[4,64,1024]{2,1,0:T(8,128)(2,1)S(1)} %stack.2.own), channel_id=1, source_target_pairs={{0,4},{1,5},{2,6},{3,7},{4,8},{5,9},{6,10},{7,11},{8,12},{9,13},{1... | collective-permute-start | bytes 1572872 | tf_op jit(solution)/shard_map/ppermute | solution.py:250
  21.2 5.7 %collective-permute-start.10 = (bf16[256,2048]{1,0:T(8,128)(2,1)S(1)}, bf16[256,2048]{1,0:T(8,128)(2,1)S(1)}, u32[]{:S(2)}, u32[]{:S(2)}) collective-permute-start(bf16[256,2048]{1,0:T(8,128)(2,1)S(1)} %get-tuple-element.17.rows), channel_id=1, source_target_pairs={{0,16},{16,0},{32,48},{48,32},{64,80},{80,64},{96,112},{112,96},{1... | collective-permute-start | bytes 3145736 | tf_op jit(solution)/shard_map/ppermute | solution.py:241
  21.3 10.6 %collective-permute-start.9 = (bf16[128,2048]{1,0:T(8,128)(2,1)S(1)}, bf16[128,2048]{1,0:T(8,128)(2,1)S(1)}, u32[]{:S(2)}, u32[]{:S(2)}) collective-permute-start(bf16[128,2048]{1,0:T(8,128)(2,1)S(1)} %get-tuple-element.16), channel_id=1, source_target_pairs={{0,32},{16,112},{32,64},{48,16},{64,96},{80,48},{96,0},{112,80},{1... | collective-permute-start | bytes 1572872 | tf_op jit(solution)/shard_map/ppermute | solution.py:253
  32.0 3.1 %collective-permute-start.11 = (bf16[128,2048]{1,0:T(8,128)(2,1)S(1)}, bf16[128,2048]{1,0:T(8,128)(2,1)S(1)}, u32[]{:S(2)}, u32[]{:S(2)}) collective-permute-start(bf16[128,2048]{1,0:T(8,128)(2,1)S(1)} %bitcast.1), channel_id=1, source_target_pairs={{0,16},{16,0},{32,48},{48,32},{64,80},{80,64},{96,112},{112,96},{1... | collective-permute-start | bytes 1572872 | tf_op jit(solution)/shard_map/ppermute | solution.py:241
  35.1 5.0 %copy-start.1 = (s32[16]{0:T(128)S(1)}, s32[16]{0:T(128)}, u32[]{:S(2)}) copy-start(s32[16]{0:T(128)} %seq_start.1) | copy-start | bytes 196
  35.1 5.0 %copy-start.2 = (s32[16]{0:T(128)S(1)}, s32[16]{0:T(128)}, u32[]{:S(2)}) copy-start(s32[16]{0:T(128)} %seq_len.1) | copy-start | bytes 196

commit v3 on v2

--- a/solution.py
+++ b/solution.py
@@ -37,6 +37,7 @@
 
 
 OTHER_CORE = [(i, i ^ 1) for i in range(8)]
+SAME_CORE = [[16 * row + col for row in range(core, 8, 2) for col in range(16)] for core in range(2)]
 Y_BY_CORE = [(i, (i + 2 - 4 * (i % 2)) % 8) for i in range(8)]
 
 
@@ -228,9 +229,10 @@
     )(seq_start, seq_len, *acts, resident(products))
 
 
-def from_all(value, axis):
-    copies = jnp.broadcast_to(value[None], (lax.axis_size(axis),) + value.shape)
-    return lax.all_to_all(copies, axis, 0, 0, tiled=True)
+def total(value):
+    value = value + lax.ppermute(value, "row", OTHER_CORE)
+    copies = jnp.broadcast_to(value[None], (len(SAME_CORE[0]),) + value.shape)
+    return jnp.sum(lax.all_to_all(copies, ("row", "col"), 0, 0, axis_index_groups=SAME_CORE, tiled=True), axis=0)
 
 
 def on_device(activations, out_grads, queries, seq_start, seq_len):
@@ -260,8 +262,7 @@
     products, token = next_products("other_high", places, pair_other, held, products, (nq // 2, nq))
     products, token = next_products("far", [(2, 0), (2, 1)], join(far, far_other), held, products, (0, nq))
     scores = partial_scores(seq_start, seq_len, acts, products)
-    scores = jnp.sum(from_all(scores, "row"), axis=0)
-    return jnp.sum(from_all(scores, "col"), axis=0)
+    return total(scores)
 
 
 def solution(mesh):

time: 64.4 us -> 61.7 us (0.958)
  blocking collectives: 20.6 us -> 16.5 us
  waiting for transfers between devices: 2.7 us -> 3.52 us
    all_to_all x2 -> x1, blocking collectives: 20.6 us -> 16.5 us  [total(): lax.all_to_all(copies, ('row', 'col'), 0, 0, axis_index_groups=SAME_CORE,...]
    ppermute x0 -> x1, waiting for transfers between devices: none -> 0.82 us  [total(): value = value + lax.ppermute(value, 'row', OTHER_CORE)]
  transfers between devices with their start and end apart: 12 -> 13, of which waited for: 1 -> 2; matrix products, arithmetic and copies ran while one was open for 0% -> 0% of each run, Pallas kernels for 36% -> 38%
where the time goes in v3:
time: 61.7 us; the launch traced here: 61.5 us
  Pallas kernels  25.9 us (42%)
  blocking collectives  16.5 us (27%)
  starting transfers between devices  14.7 us (24%)
  waiting for transfers between devices  3.52 us (6%)
  other arithmetic  0.66 us (1%)
    all_to_all x1, blocking collectives, total(): lax.all_to_all(copies, ('row', 'col'), 0, 0, axis_index_groups=SAME_CORE,...  16.5 us
    pallas_call x4, Pallas kernels, next_products(): pl.pallas_call(functools.partial(next_kernel, places, computed), in_specs...  15.1 us
    pallas_call x1, Pallas kernels, near_products(): pl.pallas_call(functools.partial(near_kernel, places), in_specs=[HBM, VME...  7.78 us
    ppermute x3, starting transfers between devices, on_device(): lax.ppermute(activations, ('row', 'col'), along_both(along_z, along_x, -d))  5.42 us
    ppermute x3, starting transfers between devices, on_device(): lax.ppermute(own_act, ('row', 'col'), along_both(along_x, along_z, -d))  4.51 us
    pallas_call x1, Pallas kernels, partial_scores(): pl.pallas_call(score_kernel, in_specs=[SMEM] * 2 + [VMEM] * (len(acts) +...  2.84 us
    ppermute x1, waiting for transfers between devices, on_device(): far = lax.ppermute(onward, 'row', Y_BY_CORE)  2.67 us
    ppermute x1, starting transfers between devices, on_device(): below = lax.ppermute(out_grads, 'row', along_y(1))  1.72 us
  transfers between devices with their start and end apart: 13, of which 2 were waited for; matrix products, arithmetic and copies ran while one was open for 0% of the time, Pallas kernels for 38%

profile of v3, /device:TPU:0, one launch (start us, length us, event | category | flops | bytes accessed | tf_op | source)
XLA Modules:
  0.0 61.5 jit_solution(15111564779460522639)
XLA Ops:
  0.0 0.0 collective-permute-start.3
  0.0 1.7 %collective-permute-start.7 = (bf16[128,2048]{1,0:T(8,128)(2,1)}, bf16[128,2048]{1,0:T(8,128)(2,1)S(1)}, u32[]{:S(2)}, u32[]{:S(2)}) collective-permute-start(bf16[128,2048]{1,0:T(8,128)(2,1)} %own.1), channel_id=1, source_target_pairs={{0,32},{16,48},{32,64},{48,80},{64,96},{80,112},{96,0},{112,16},{1... | collective-permute-start | bytes 1572872 | tf_op jit(solution)/shard_map/ppermute | solution.py:245
  1.7 1.5 %collective-permute-start.8 = (bf16[128,2048]{1,0:T(8,128)(2,1)}, bf16[128,2048]{1,0:T(8,128)(2,1)S(1)}, u32[]{:S(2)}, u32[]{:S(2)}) collective-permute-start(bf16[128,2048]{1,0:T(8,128)(2,1)} %own.1), channel_id=1, source_target_pairs={{0,96},{16,112},{32,0},{48,16},{64,32},{80,48},{96,64},{112,80},{1... | collective-permute-start | bytes 1572872 | tf_op jit(solution)/shard_map/ppermute | solution.py:246
  3.3 4.2 %collective-permute-start = (bf16[64,1024]{1,0:T(8,128)(2,1)}, bf16[64,1024]{1,0:T(8,128)(2,1)S(1)}, u32[]{:S(2)}, u32[]{:S(2)}) collective-permute-start(bf16[64,1024]{1,0:T(8,128)(2,1)} %refs_0_.1), channel_id=1, source_target_pairs={{0,3},{1,0},{2,1},{3,2},{4,7},{5,4},{6,5},{7,6},{8,11},{9,8},{10,9... | collective-permute-start | bytes 393224 | tf_op jit(solution)/shard_map/ppermute | solution.py:248
  7.4 0.0 collective-permute-done.3.other
  7.4 1.3 %collective-permute-start.2 = (bf16[64,1024]{1,0:T(8,128)(2,1)}, bf16[64,1024]{1,0:T(8,128)(2,1)S(1)}, u32[]{:S(2)}, u32[]{:S(2)}) collective-permute-start(bf16[64,1024]{1,0:T(8,128)(2,1)} %refs_0_.1), channel_id=1, source_target_pairs={{0,1},{1,2},{2,3},{3,0},{4,5},{5,6},{6,7},{7,4},{8,9},{9,10},{10,1... | collective-permute-start | bytes 393224 | tf_op jit(solution)/shard_map/ppermute | solution.py:248
  8.7 7.8 %near.1 = (f32[4,1024,1024]{2,1,0:T(8,128)S(1)}, bf16[4,1024,2048]{2,1,0:T(8,128)(2,1)S(1)}, f32[8,128]{1,0:T(8,128)S(1)}) custom-call(bf16[128,2048]{1,0:T(8,128)(2,1)} %own.1, bf16[128,2048]{1,0:T(8,128)(2,1)S(1)} %collective-permute-done.3.other, bf16[4,1024,2048]{2,1,0:T(8,128)(2,1)} %queries.1), custom_call_target="tpu_custom_call" | custom-call | flops 42949672960 | bytes 16777216 | tf_op jit(solution)/shard_map/near/pallas_call | solution.py:89
  16.5 0.0 collective-permute-done.refs_1_
  16.5 0.0 collective-permute-done.1.refs_2_
  16.6 2.8 %collective-permute-start.4 = (bf16[4,64,1024]{2,1,0:T(8,128)(2,1)S(1)}, bf16[4,64,1024]{2,1,0:T(8,128)(2,1)S(1)}, u32[]{:S(2)}, u32[]{:S(2)}) collective-permute-start(bf16[4,64,1024]{2,1,0:T(8,128)(2,1)S(1)} %stack.2.own), channel_id=1, source_target_pairs={{0,12},{1,13},{2,14},{3,15},{4,0},{5,1},{6,2},{7,3},{8,4},{9,5},{1... | collective-permute-start | bytes 1572872 | tf_op jit(solution)/shard_map/ppermute | solution.py:252
  19.4 0.8 %collective-permute-start.5 = (bf16[4,64,1024]{2,1,0:T(8,128)(2,1)S(1)}, bf16[4,64,1024]{2,1,0:T(8,128)(2,1)S(1)}, u32[]{:S(2)}, u32[]{:S(2)}) collective-permute-start(bf16[4,64,1024]{2,1,0:T(8,128)(2,1)S(1)} %stack.2.own), channel_id=1, source_target_pairs={{0,8},{1,9},{2,10},{3,11},{4,12},{5,13},{6,14},{7,15},{8,0},{9,1},... | collective-permute-start | bytes 1572872 | tf_op jit(solution)/shard_map/ppermute | solution.py:252
  20.2 0.9 %collective-permute-start.6 = (bf16[4,64,1024]{2,1,0:T(8,128)(2,1)S(1)}, bf16[4,64,1024]{2,1,0:T(8,128)(2,1)S(1)}, u32[]{:S(2)}, u32[]{:S(2)}) collective-permute-start(bf16[4,64,1024]{2,1,0:T(8,128)(2,1)S(1)} %stack.2.own), channel_id=1, source_target_pairs={{0,4},{1,5},{2,6},{3,7},{4,8},{5,9},{6,10},{7,11},{8,12},{9,13},{1... | collective-permute-start | bytes 1572872 | tf_op jit(solution)/shard_map/ppermute | solution.py:252
  21.1 0.0 collective-permute-done.7.below
  21.1 0.0 collective-permute-done.8.above
  21.1 0.1 pair.1
  21.2 0.1 collective-permute-start.10
  21.3 0.6 collective-permute-start.9
  21.9 5.0 %mid.1 = (f32[4,1024,1024]{2,1,0:T(8,128)S(1)}, f32[8,128]{1,0:T(8,128)}) custom-call(bf16[256,2048]{1,0:T(8,128)(2,1)S(1)} %get-tuple-element.17.rows, bf16[4,1024,2048]{2,1,0:T(8,128)(2,1)S(1)} %get-tuple-element.18.held, f32[4,1024,1024]{2,1,0:T(8,128)S(1)} %get-tuple-element.19._), custom_call_target="tpu_custom_call", output_to_operand_aliasing={{0}: (2, {})} | custom-call | flops 42949672960 | bytes 1048576 | tf_op jit(solution)/shard_map/mid/pallas_call | solution.py:112
  26.9 0.0 collective-permute-done.10.rows
  26.9 2.4 %other_low.1 = (f32[4,1024,1024]{2,1,0:T(8,128)S(1)}, f32[8,128]{1,0:T(8,128)S(1)}) custom-call(bf16[256,2048]{1,0:T(8,128)(2,1)S(1)} %collective-permute-done.10.rows, bf16[4,1024,2048]{2,1,0:T(8,128)(2,1)S(1)} %get-tuple-element.18.held, f32[4,1024,1024]{2,1,0:T(8,128)S(1)} %get-tuple-element.20._), custom_call_target="tpu_custom_call", output_to_operand_aliasing={{0}: (2, {})} | custom-call | flops 21474836480 | bytes 1048576 | tf_op jit(solution)/shard_map/other_low/pallas_call | solution.py:112
  29.3 2.7 %collective-permute-done.9.refs_0_ = bf16[128,2048]{1,0:T(8,128)(2,1)S(1)} collective-permute-done((bf16[128,2048]{1,0:T(8,128)(2,1)S(1)}, bf16[128,2048]{1,0:T(8,128)(2,1)S(1)}, u32[]{:S(2)}, u32[]{:S(2)}) %collective-permute-start.9) | collective-permute-done | bytes 524320 | tf_op jit(solution)/shard_map/ppermute | solution.py:255
  32.0 0.3 collective-permute-start.11
  32.3 2.8 %other_high.1 = (f32[4,1024,1024]{2,1,0:T(8,128)S(1)}, f32[8,128]{1,0:T(8,128)}) custom-call(bf16[256,2048]{1,0:T(8,128)(2,1)S(1)} %collective-permute-done.10.rows, bf16[4,1024,2048]{2,1,0:T(8,128)(2,1)S(1)} %get-tuple-element.18.held, f32[4,1024,1024]{2,1,0:T(8,128)S(1)} %get-tuple-element.22._), custom_call_target="tpu_custom_call", output_to_operand_aliasing={{0}: (2, {})} | custom-call | flops 21474836480 | bytes 1048576 | tf_op jit(solution)/shard_map/other_high/pallas_call | solution.py:112
  35.1 0.1 join.1.rows
  35.1 0.0 copy-start.1
  35.1 0.0 copy-start.2
  35.1 5.0 %far.1 = (f32[4,1024,1024]{2,1,0:T(8,128)S(1)}, f32[8,128]{1,0:T(8,128)}) custom-call(bf16[256,2048]{1,0:T(8,128)(2,1)S(1)} %join.1.rows, bf16[4,1024,2048]{2,1,0:T(8,128)(2,1)S(1)} %get-tuple-element.18.held, f32[4,1024,1024]{2,1,0:T(8,128)S(1)} %get-tuple-element.23._), custom_call_target="tpu_custom_call", output_to_operand_aliasing={{0}: (2, {})} | custom-call | flops 42949672960 | bytes 1048576 | tf_op jit(solution)/shard_map/far/pallas_call | solution.py:112
  40.1 2.8 %scores.1 = f32[4,16]{1,0:T(4,128)S(1)} custom-call(s32[16]{0:T(128)S(1)} %copy-done.1, s32[16]{0:T(128)S(1)} %copy-done.2, bf16[4,64,1024]{2,1,0:T(8,128)(2,1)S(1)} %stack.2.own, bf16[4,64,1024]{2,1,0:T(8,128)(2,1)S(1)} %collective-permute-done.4.ahead, bf16[4,64,1024]{2,1,0:T(8,128)(2,1)S(1)} %collective-permute-done.5.far, ...), custom_call_target="tpu_custom_call" | custom-call | flops 1073741824 | bytes 4194304 | tf_op jit(solution)/shard_map/scores/pallas_call | solution.py:220
  43.0 0.5 collective-permute-start.12
  43.5 0.8 %collective-permute-done.12 = f32[4,16]{1,0:T(4,128)S(1)} collective-permute-done((f32[4,16]{1,0:T(4,128)S(1)}, f32[4,16]{1,0:T(4,128)S(1)}, u32[]{:S(2)}, u32[]{:S(2)}) %collective-permute-start.12) | collective-permute-done | bytes 288 | tf_op jit(solution)/shard_map/ppermute | solution.py:233
  44.3 16.5 %all_to_all.5 = f32[64,4,16]{2,1,0:T(4,128)S(1)} all-to-all(f32[64,4,16]{2,1,0:T(4,128)S(1)} %broadcast_in_dim.2), channel_id=1, replica_groups={{0,1,2,3,4,5,6,7,8,9,10,11,12,13,14,15,32,33,34,35,36,37,38,39,40,41,42..., dimensions={0} | all-to-all | bytes 32768 | tf_op jit(solution)/shard_map/all_to_all | solution.py:235
  60.9 0.7 %reduce_sum.9 = f32[4,16]{1,0:T(4,128)} reduce(f32[64,4,16]{2,1,0:T(4,128)S(1)} %all_to_all.5, f32[]{:T(128)} %constant.0.clone.1), dimensions={0}, to_apply=%region_0.0 | reduce | flops 4032 | bytes 16644 | tf_op jit(solution)/shard_map/reduce_sum | solution.py:235
  (14 shorter events, 0.1 us)
Async XLA Ops:
  0.0 16.5 %copy-start = (bf16[64,1024]{1,0:T(8,128)(2,1)S(1)}, bf16[64,1024]{1,0:T(8,128)(2,1)}, u32[]{:S(2)}) copy-start(bf16[64,1024]{1,0:T(8,128)(2,1)} %refs_0_.1) | copy-start | bytes 393220
  0.0 7.4 %collective-permute-start.3 = (bf16[128,2048]{1,0:T(8,128)(2,1)}, bf16[128,2048]{1,0:T(8,128)(2,1)S(1)}, u32[]{:S(2)}, u32[]{:S(2)}) collective-permute-start(bf16[128,2048]{1,0:T(8,128)(2,1)} %own.1), channel_id=1, source_target_pairs={{0,16},{16,0},{32,48},{48,32},{64,80},{80,64},{96,112},{112,96},{1... | collective-permute-start | bytes 1572872 | tf_op jit(solution)/shard_map/ppermute | solution.py:243
  0.0 21.1 %collective-permute-start.7 = (bf16[128,2048]{1,0:T(8,128)(2,1)}, bf16[128,2048]{1,0:T(8,128)(2,1)S(1)}, u32[]{:S(2)}, u32[]{:S(2)}) collective-permute-start(bf16[128,2048]{1,0:T(8,128)(2,1)} %own.1), channel_id=1, source_target_pairs={{0,32},{16,48},{32,64},{48,80},{64,96},{80,112},{96,0},{112,16},{1... | collective-permute-start | bytes 1572872 | tf_op jit(solution)/shard_map/ppermute | solution.py:245
  1.7 19.4 %collective-permute-start.8 = (bf16[128,2048]{1,0:T(8,128)(2,1)}, bf16[128,2048]{1,0:T(8,128)(2,1)S(1)}, u32[]{:S(2)}, u32[]{:S(2)}) collective-permute-start(bf16[128,2048]{1,0:T(8,128)(2,1)} %own.1), channel_id=1, source_target_pairs={{0,96},{16,112},{32,0},{48,16},{64,32},{80,48},{96,64},{112,80},{1... | collective-permute-start | bytes 1572872 | tf_op jit(solution)/shard_map/ppermute | solution.py:246
  3.3 13.2 %collective-permute-start = (bf16[64,1024]{1,0:T(8,128)(2,1)}, bf16[64,1024]{1,0:T(8,128)(2,1)S(1)}, u32[]{:S(2)}, u32[]{:S(2)}) collective-permute-start(bf16[64,1024]{1,0:T(8,128)(2,1)} %refs_0_.1), channel_id=1, source_target_pairs={{0,3},{1,0},{2,1},{3,2},{4,7},{5,4},{6,5},{7,6},{8,11},{9,8},{10,9... | collective-permute-start | bytes 393224 | tf_op jit(solution)/shard_map/ppermute | solution.py:248
  7.4 9.1 %collective-permute-start.1 = (bf16[64,1024]{1,0:T(8,128)(2,1)}, bf16[64,1024]{1,0:T(8,128)(2,1)S(1)}, u32[]{:S(2)}, u32[]{:S(2)}) collective-permute-start(bf16[64,1024]{1,0:T(8,128)(2,1)} %refs_0_.1), channel_id=1, source_target_pairs={{0,2},{1,3},{2,0},{3,1},{4,6},{5,7},{6,4},{7,5},{8,10},{9,11},{10,... | collective-permute-start | bytes 393224 | tf_op jit(solution)/shard_map/ppermute | solution.py:248
  7.4 9.1 %collective-permute-start.2 = (bf16[64,1024]{1,0:T(8,128)(2,1)}, bf16[64,1024]{1,0:T(8,128)(2,1)S(1)}, u32[]{:S(2)}, u32[]{:S(2)}) collective-permute-start(bf16[64,1024]{1,0:T(8,128)(2,1)} %refs_0_.1), channel_id=1, source_target_pairs={{0,1},{1,2},{2,3},{3,0},{4,5},{5,6},{6,7},{7,4},{8,9},{9,10},{10,1... | collective-permute-start | bytes 393224 | tf_op jit(solution)/shard_map/ppermute | solution.py:248
  16.6 23.5 %collective-permute-start.4 = (bf16[4,64,1024]{2,1,0:T(8,128)(2,1)S(1)}, bf16[4,64,1024]{2,1,0:T(8,128)(2,1)S(1)}, u32[]{:S(2)}, u32[]{:S(2)}) collective-permute-start(bf16[4,64,1024]{2,1,0:T(8,128)(2,1)S(1)} %stack.2.own), channel_id=1, source_target_pairs={{0,12},{1,13},{2,14},{3,15},{4,0},{5,1},{6,2},{7,3},{8,4},{9,5},{1... | collective-permute-start | bytes 1572872 | tf_op jit(solution)/shard_map/ppermute | solution.py:252
  19.4 20.7 %collective-permute-start.5 = (bf16[4,64,1024]{2,1,0:T(8,128)(2,1)S(1)}, bf16[4,64,1024]{2,1,0:T(8,128)(2,1)S(1)}, u32[]{:S(2)}, u32[]{:S(2)}) collective-permute-start(bf16[4,64,1024]{2,1,0:T(8,128)(2,1)S(1)} %stack.2.own), channel_id=1, source_target_pairs={{0,8},{1,9},{2,10},{3,11},{4,12},{5,13},{6,14},{7,15},{8,0},{9,1},... | collective-permute-start | bytes 1572872 | tf_op jit(solution)/shard_map/ppermute | solution.py:252
  20.2 19.9 %collective-permute-start.6 = (bf16[4,64,1024]{2,1,0:T(8,128)(2,1)S(1)}, bf16[4,64,1024]{2,1,0:T(8,128)(2,1)S(1)}, u32[]{:S(2)}, u32[]{:S(2)}) collective-permute-start(bf16[4,64,1024]{2,1,0:T(8,128)(2,1)S(1)} %stack.2.own), channel_id=1, source_target_pairs={{0,4},{1,5},{2,6},{3,7},{4,8},{5,9},{6,10},{7,11},{8,12},{9,13},{1... | collective-permute-start | bytes 1572872 | tf_op jit(solution)/shard_map/ppermute | solution.py:252
  21.2 5.7 %collective-permute-start.10 = (bf16[256,2048]{1,0:T(8,128)(2,1)S(1)}, bf16[256,2048]{1,0:T(8,128)(2,1)S(1)}, u32[]{:S(2)}, u32[]{:S(2)}) collective-permute-start(bf16[256,2048]{1,0:T(8,128)(2,1)S(1)} %get-tuple-element.17.rows), channel_id=1, source_target_pairs={{0,16},{16,0},{32,48},{48,32},{64,80},{80,64},{96,112},{112,96},{1... | collective-permute-start | bytes 3145736 | tf_op jit(solution)/shard_map/ppermute | solution.py:243
  21.3 10.6 %collective-permute-start.9 = (bf16[128,2048]{1,0:T(8,128)(2,1)S(1)}, bf16[128,2048]{1,0:T(8,128)(2,1)S(1)}, u32[]{:S(2)}, u32[]{:S(2)}) collective-permute-start(bf16[128,2048]{1,0:T(8,128)(2,1)S(1)} %get-tuple-element.16), channel_id=1, source_target_pairs={{0,32},{16,112},{32,64},{48,16},{64,96},{80,48},{96,0},{112,80},{1... | collective-permute-start | bytes 1572872 | tf_op jit(solution)/shard_map/ppermute | solution.py:255
  32.0 3.1 %collective-permute-start.11 = (bf16[128,2048]{1,0:T(8,128)(2,1)S(1)}, bf16[128,2048]{1,0:T(8,128)(2,1)S(1)}, u32[]{:S(2)}, u32[]{:S(2)}) collective-permute-start(bf16[128,2048]{1,0:T(8,128)(2,1)S(1)} %bitcast.1), channel_id=1, source_target_pairs={{0,16},{16,0},{32,48},{48,32},{64,80},{80,64},{96,112},{112,96},{1... | collective-permute-start | bytes 1572872 | tf_op jit(solution)/shard_map/ppermute | solution.py:243
  35.1 5.0 %copy-start.1 = (s32[16]{0:T(128)S(1)}, s32[16]{0:T(128)}, u32[]{:S(2)}) copy-start(s32[16]{0:T(128)} %seq_start.1) | copy-start | bytes 196
  35.1 5.0 %copy-start.2 = (s32[16]{0:T(128)S(1)}, s32[16]{0:T(128)}, u32[]{:S(2)}) copy-start(s32[16]{0:T(128)} %seq_len.1) | copy-start | bytes 196
  43.0 1.3 %collective-permute-start.12 = (f32[4,16]{1,0:T(4,128)S(1)}, f32[4,16]{1,0:T(4,128)S(1)}, u32[]{:S(2)}, u32[]{:S(2)}) collective-permute-start(f32[4,16]{1,0:T(4,128)S(1)} %scores.1), channel_id=1, source_target_pairs={{0,16},{16,0},{32,48},{48,32},{64,80},{80,64},{96,112},{112,96},{1... | collective-permute-start | bytes 776 | tf_op jit(solution)/shard_map/ppermute | solution.py:233

commit v4 on v3

--- a/solution.py
+++ b/solution.py
@@ -10,6 +10,7 @@
 NT = (((1,), (1,)), ((), ()))
 SLOT = 64
 BLOCK = 128
+PART = 16
 VMEM = pl.BlockSpec(memory_space=pltpu.VMEM)
 SMEM = pl.BlockSpec(memory_space=pltpu.SMEM)
 HBM = pl.BlockSpec(memory_space=pltpu.HBM)
@@ -55,20 +56,13 @@
     return pl.multiple_of((y + dy) % 4 * 2 * BLOCK + (core + dcore) % 2 * BLOCK, BLOCK)
 
 
-def store_products(result, products, places, q, columns=slice(None)):
+def store_products(result, products, places, q):
     for i, (dy, dcore) in enumerate(places):
-        products[q, pl.ds(first_row(dy, dcore), BLOCK), columns] = result[i * BLOCK : (i + 1) * BLOCK]
+        products[q, pl.ds(first_row(dy, dcore), BLOCK), :] = result[i * BLOCK : (i + 1) * BLOCK]
 
 
 def near_kernel(places, own, other, queries, products, held, token, rows, sems):
-    nq, width, _ = held.shape
-    half = width // 2
-    chunks = [(0, slice(0, half)), (0, slice(half, width))]
-    chunks += [(q, slice(0, width)) for q in range(1, nq - 1)]
-    chunks += [(nq - 1, slice(0, half)), (nq - 1, slice(half, width))]
-    copies = [
-        pltpu.make_async_copy(queries.at[q, part], held.at[q, part], sems.at[i]) for i, (q, part) in enumerate(chunks)
-    ]
+    copies = [pltpu.make_async_copy(queries.at[q], held.at[q], sems.at[q]) for q in range(held.shape[0])]
     block_copies = [
         pltpu.make_async_copy(block, rows.at[pl.ds(i * BLOCK, BLOCK)], sems.at[len(copies) + i])
         for i, block in enumerate((own, other))
@@ -78,10 +72,10 @@
     token[...] = jnp.zeros_like(token)
     for copy in block_copies:
         copy.wait()
-    for copy, (q, part) in zip(copies, chunks, strict=True):
+    for q, copy in enumerate(copies):
         copy.wait()
-        result = lax.dot_general(rows[...], held[q, part], NT, preferred_element_type=jnp.float32)
-        store_products(result, products, places, q, part)
+        result = lax.dot_general(rows[...], held[q], NT, preferred_element_type=jnp.float32)
+        store_products(result, products, places, q)
 
 
 def near_products(places, own, other, queries, tokens):
@@ -91,7 +85,7 @@
         in_specs=[HBM, VMEM, HBM],
         out_specs=[VMEM] * 3,
         out_shape=[pltpu.VMEM((nq, tokens, width), jnp.float32), pltpu.VMEM(queries.shape, queries.dtype), TOKEN],
-        scratch_shapes=[pltpu.VMEM((2 * BLOCK, depth), own.dtype), pltpu.SemaphoreType.DMA((2 * nq + 2,))],
+        scratch_shapes=[pltpu.VMEM((2 * BLOCK, depth), own.dtype), pltpu.SemaphoreType.DMA((nq + 2,))],
         compiler_params=SMALL,
         cost_estimate=pl.CostEstimate(
             flops=WEIGHT * 4 * BLOCK * queries.size, bytes_accessed=2 * queries.size, transcendentals=0
@@ -185,7 +179,7 @@
 def score_kernel(seq_start, seq_len, own, ahead, far, behind, products, out, lanes):
     col = lax.axis_index("col")
     x, z, core = col // 4, col % 4, my_core()
-    nq = out.shape[0]
+    nq = products.shape[0]
     width = products.shape[2]
     position = lax.broadcasted_iota(jnp.int32, (SLOT, 128), 0)
     for d, block in enumerate((own, ahead, far, behind)):
@@ -197,21 +191,24 @@
             token = position + base
             start = seq_start[slot]
             inside = (token >= start) & (token < start + seq_len[slot])
-            totals = [jnp.zeros((SLOT, 128), jnp.float32) for _ in range(nq)]
-            for w in range(0, width, 128):
-                act = block[i, :, w : w + 128].astype(jnp.float32)
+            kept = [jnp.zeros((PART, 128), jnp.float32) for _ in range(nq)]
+            for part in range(0, SLOT, PART):
+                totals = [jnp.zeros((PART, 128), jnp.float32) for _ in range(nq)]
+                for w in range(0, width, 128):
+                    act = block[i, part : part + PART, w : w + 128].astype(jnp.float32)
+                    for q in range(nq):
+                        totals[q] += products[q, pl.ds(base + part, PART), w : w + 128] * act
                 for q in range(nq):
-                    totals[q] += products[q, pl.ds(base, SLOT), w : w + 128] * act
+                    kept[q] += jnp.where(inside[part : part + PART], totals[q], 0.0)
             for q in range(nq):
-                kept = jnp.where(inside, totals[q], 0.0)
-                lanes[q, pl.ds(slot, 1), :] = jnp.sum(kept, axis=0, keepdims=True)
+                lanes[q, pl.ds(slot, 1), :] = jnp.sum(kept[q], axis=0, keepdims=True)
             return carry
 
         lax.fori_loop(0, 4, one_slot, 0)
     ones = jnp.ones((8, 128), jnp.float32)
-    for q in range(nq):
-        sums = lax.dot_general(ones, lanes[q], NT, precision=lax.Precision.HIGHEST, preferred_element_type=jnp.float32)
-        out[q : q + 1, :] = sums[:1, :]
+    rows = lanes[...].reshape(nq * lanes.shape[1], 128)
+    sums = lax.dot_general(ones, rows, NT, precision=lax.Precision.HIGHEST, preferred_element_type=jnp.float32)
+    out[...] = sums[:1, :]
 
 
 def partial_scores(seq_start, seq_len, acts, products):
@@ -221,7 +218,7 @@
         score_kernel,
         in_specs=[SMEM] * 2 + [VMEM] * (len(acts) + 1),
         out_specs=VMEM,
-        out_shape=jax.ShapeDtypeStruct((nq, nseq), jnp.float32),
+        out_shape=jax.ShapeDtypeStruct((1, nq * nseq), jnp.float32),
         scratch_shapes=[pltpu.VMEM((nq, nseq, 128), jnp.float32)],
         compiler_params=SMALL,
         cost_estimate=pl.CostEstimate(flops=1 << 30, bytes_accessed=4 << 20, transcendentals=0),
@@ -262,7 +259,7 @@
     products, token = next_products("other_high", places, pair_other, held, products, (nq // 2, nq))
     products, token = next_products("far", [(2, 0), (2, 1)], join(far, far_other), held, products, (0, nq))
     scores = partial_scores(seq_start, seq_len, acts, products)
-    return total(scores)
+    return total(scores).reshape(queries.shape[0], seq_start.shape[0])
 
 
 def solution(mesh):

time: 61.7 us -> 60.9 us (0.987)
  local copies, waits for them, and re-layouts: 0.04 us -> 0.7 us
  other arithmetic: 0.66 us -> 0.03 us
    reshape x0 -> x1, local copies, waits for them, and re-layouts: none -> 0.66 us  [on_device(): return total(scores).reshape(queries.shape[0], seq_start.shape[0])]
    reduce_sum x1, other arithmetic: 0.65 us -> 0.03 us  [total(): jnp.sum(lax.all_to_all(copies, ('row', 'col'), 0, 0, axis_index_groups=SA...]
where the time goes in v4:
time: 60.9 us; the launch traced here: 60.8 us
  Pallas kernels  25.5 us (42%)
  blocking collectives  16.1 us (26%)
  starting transfers between devices  14.7 us (24%)
  waiting for transfers between devices  3.52 us (6%)
  local copies, waits for them, and re-layouts  0.7 us (1%)
    all_to_all x1, blocking collectives, total(): lax.all_to_all(copies, ('row', 'col'), 0, 0, axis_index_groups=SAME_CORE,...  16.1 us
    pallas_call x4, Pallas kernels, next_products(): pl.pallas_call(functools.partial(next_kernel, places, computed), in_specs...  15.1 us
    pallas_call x1, Pallas kernels, near_products(): pl.pallas_call(functools.partial(near_kernel, places), in_specs=[HBM, VME...  7.54 us
    ppermute x3, starting transfers between devices, on_device(): lax.ppermute(activations, ('row', 'col'), along_both(along_z, along_x, -d))  5.42 us
    ppermute x3, starting transfers between devices, on_device(): lax.ppermute(own_act, ('row', 'col'), along_both(along_x, along_z, -d))  4.51 us
    ppermute x1, waiting for transfers between devices, on_device(): far = lax.ppermute(onward, 'row', Y_BY_CORE)  2.67 us
    pallas_call x1, Pallas kernels, partial_scores(): pl.pallas_call(score_kernel, in_specs=[SMEM] * 2 + [VMEM] * (len(acts) +...  2.65 us
    ppermute x1, starting transfers between devices, on_device(): below = lax.ppermute(out_grads, 'row', along_y(1))  1.72 us
  transfers between devices with their start and end apart: 13, of which 2 were waited for; matrix products, arithmetic and copies ran while one was open for 0% of the time, Pallas kernels for 38%

profile of v4, /device:TPU:0, one launch (start us, length us, event | category | flops | bytes accessed | tf_op | source)
XLA Modules:
  0.0 60.8 jit_solution(13129477817658146244)
XLA Ops:
  0.0 0.0 collective-permute-start.3
  0.0 1.7 %collective-permute-start.7 = (bf16[128,2048]{1,0:T(8,128)(2,1)}, bf16[128,2048]{1,0:T(8,128)(2,1)S(1)}, u32[]{:S(2)}, u32[]{:S(2)}) collective-permute-start(bf16[128,2048]{1,0:T(8,128)(2,1)} %own.1), channel_id=1, source_target_pairs={{0,32},{16,48},{32,64},{48,80},{64,96},{80,112},{96,0},{112,16},{1... | collective-permute-start | bytes 1572872 | tf_op jit(solution)/shard_map/ppermute | solution.py:242
  1.7 1.5 %collective-permute-start.8 = (bf16[128,2048]{1,0:T(8,128)(2,1)}, bf16[128,2048]{1,0:T(8,128)(2,1)S(1)}, u32[]{:S(2)}, u32[]{:S(2)}) collective-permute-start(bf16[128,2048]{1,0:T(8,128)(2,1)} %own.1), channel_id=1, source_target_pairs={{0,96},{16,112},{32,0},{48,16},{64,32},{80,48},{96,64},{112,80},{1... | collective-permute-start | bytes 1572872 | tf_op jit(solution)/shard_map/ppermute | solution.py:243
  3.3 4.2 %collective-permute-start = (bf16[64,1024]{1,0:T(8,128)(2,1)}, bf16[64,1024]{1,0:T(8,128)(2,1)S(1)}, u32[]{:S(2)}, u32[]{:S(2)}) collective-permute-start(bf16[64,1024]{1,0:T(8,128)(2,1)} %refs_0_.1), channel_id=1, source_target_pairs={{0,3},{1,0},{2,1},{3,2},{4,7},{5,4},{6,5},{7,6},{8,11},{9,8},{10,9... | collective-permute-start | bytes 393224 | tf_op jit(solution)/shard_map/ppermute | solution.py:245
  7.4 0.0 collective-permute-start.1
  7.4 0.0 collective-permute-done.3.other
  7.4 1.3 %collective-permute-start.2 = (bf16[64,1024]{1,0:T(8,128)(2,1)}, bf16[64,1024]{1,0:T(8,128)(2,1)S(1)}, u32[]{:S(2)}, u32[]{:S(2)}) collective-permute-start(bf16[64,1024]{1,0:T(8,128)(2,1)} %refs_0_.1), channel_id=1, source_target_pairs={{0,1},{1,2},{2,3},{3,0},{4,5},{5,6},{6,7},{7,4},{8,9},{9,10},{10,1... | collective-permute-start | bytes 393224 | tf_op jit(solution)/shard_map/ppermute | solution.py:245
  8.7 7.5 %near.1 = (f32[4,1024,1024]{2,1,0:T(8,128)S(1)}, bf16[4,1024,2048]{2,1,0:T(8,128)(2,1)S(1)}, f32[8,128]{1,0:T(8,128)S(1)}) custom-call(bf16[128,2048]{1,0:T(8,128)(2,1)} %own.1, bf16[128,2048]{1,0:T(8,128)(2,1)S(1)} %collective-permute-done.3.other, bf16[4,1024,2048]{2,1,0:T(8,128)(2,1)} %queries.1), custom_call_target="tpu_custom_call" | custom-call | flops 42949672960 | bytes 16777216 | tf_op jit(solution)/shard_map/near/pallas_call | solution.py:83
  16.2 0.0 collective-permute-done.refs_1_
  16.3 0.0 collective-permute-done.1.refs_2_
  16.3 2.8 %collective-permute-start.4 = (bf16[4,64,1024]{2,1,0:T(8,128)(2,1)S(1)}, bf16[4,64,1024]{2,1,0:T(8,128)(2,1)S(1)}, u32[]{:S(2)}, u32[]{:S(2)}) collective-permute-start(bf16[4,64,1024]{2,1,0:T(8,128)(2,1)S(1)} %stack.2.own), channel_id=1, source_target_pairs={{0,12},{1,13},{2,14},{3,15},{4,0},{5,1},{6,2},{7,3},{8,4},{9,5},{1... | collective-permute-start | bytes 1572872 | tf_op jit(solution)/shard_map/ppermute | solution.py:249
  19.2 0.8 %collective-permute-start.5 = (bf16[4,64,1024]{2,1,0:T(8,128)(2,1)S(1)}, bf16[4,64,1024]{2,1,0:T(8,128)(2,1)S(1)}, u32[]{:S(2)}, u32[]{:S(2)}) collective-permute-start(bf16[4,64,1024]{2,1,0:T(8,128)(2,1)S(1)} %stack.2.own), channel_id=1, source_target_pairs={{0,8},{1,9},{2,10},{3,11},{4,12},{5,13},{6,14},{7,15},{8,0},{9,1},... | collective-permute-start | bytes 1572872 | tf_op jit(solution)/shard_map/ppermute | solution.py:249
  20.0 0.9 %collective-permute-start.6 = (bf16[4,64,1024]{2,1,0:T(8,128)(2,1)S(1)}, bf16[4,64,1024]{2,1,0:T(8,128)(2,1)S(1)}, u32[]{:S(2)}, u32[]{:S(2)}) collective-permute-start(bf16[4,64,1024]{2,1,0:T(8,128)(2,1)S(1)} %stack.2.own), channel_id=1, source_target_pairs={{0,4},{1,5},{2,6},{3,7},{4,8},{5,9},{6,10},{7,11},{8,12},{9,13},{1... | collective-permute-start | bytes 1572872 | tf_op jit(solution)/shard_map/ppermute | solution.py:249
  20.8 0.0 collective-permute-done.8.above
  20.9 0.1 pair.1
  21.0 0.1 collective-permute-start.10
  21.1 0.6 %collective-permute-start.9 = (bf16[128,2048]{1,0:T(8,128)(2,1)S(1)}, bf16[128,2048]{1,0:T(8,128)(2,1)S(1)}, u32[]{:S(2)}, u32[]{:S(2)}) collective-permute-start(bf16[128,2048]{1,0:T(8,128)(2,1)S(1)} %get-tuple-element.16), channel_id=1, source_target_pairs={{0,32},{16,112},{32,64},{48,16},{64,96},{80,48},{96,0},{112,80},{1... | collective-permute-start | bytes 1572872 | tf_op jit(solution)/shard_map/ppermute | solution.py:252
  21.7 5.0 %mid.1 = (f32[4,1024,1024]{2,1,0:T(8,128)S(1)}, f32[8,128]{1,0:T(8,128)}) custom-call(bf16[256,2048]{1,0:T(8,128)(2,1)S(1)} %get-tuple-element.17.rows, bf16[4,1024,2048]{2,1,0:T(8,128)(2,1)S(1)} %get-tuple-element.18.held, f32[4,1024,1024]{2,1,0:T(8,128)S(1)} %get-tuple-element.19._), custom_call_target="tpu_custom_call", output_to_operand_aliasing={{0}: (2, {})} | custom-call | flops 42949672960 | bytes 1048576 | tf_op jit(solution)/shard_map/mid/pallas_call | solution.py:106
  26.6 0.0 collective-permute-done.10.rows
  26.7 2.4 %other_low.1 = (f32[4,1024,1024]{2,1,0:T(8,128)S(1)}, f32[8,128]{1,0:T(8,128)S(1)}) custom-call(bf16[256,2048]{1,0:T(8,128)(2,1)S(1)} %collective-permute-done.10.rows, bf16[4,1024,2048]{2,1,0:T(8,128)(2,1)S(1)} %get-tuple-element.18.held, f32[4,1024,1024]{2,1,0:T(8,128)S(1)} %get-tuple-element.20._), custom_call_target="tpu_custom_call", output_to_operand_aliasing={{0}: (2, {})} | custom-call | flops 21474836480 | bytes 1048576 | tf_op jit(solution)/shard_map/other_low/pallas_call | solution.py:106
  29.0 2.7 %collective-permute-done.9.refs_0_ = bf16[128,2048]{1,0:T(8,128)(2,1)S(1)} collective-permute-done((bf16[128,2048]{1,0:T(8,128)(2,1)S(1)}, bf16[128,2048]{1,0:T(8,128)(2,1)S(1)}, u32[]{:S(2)}, u32[]{:S(2)}) %collective-permute-start.9) | collective-permute-done | bytes 524320 | tf_op jit(solution)/shard_map/ppermute | solution.py:252
  31.7 0.3 collective-permute-start.11
  32.1 2.8 %other_high.1 = (f32[4,1024,1024]{2,1,0:T(8,128)S(1)}, f32[8,128]{1,0:T(8,128)}) custom-call(bf16[256,2048]{1,0:T(8,128)(2,1)S(1)} %collective-permute-done.10.rows, bf16[4,1024,2048]{2,1,0:T(8,128)(2,1)S(1)} %get-tuple-element.18.held, f32[4,1024,1024]{2,1,0:T(8,128)S(1)} %get-tuple-element.22._), custom_call_target="tpu_custom_call", output_to_operand_aliasing={{0}: (2, {})} | custom-call | flops 21474836480 | bytes 1048576 | tf_op jit(solution)/shard_map/other_high/pallas_call | solution.py:106
  34.8 0.1 join.1.rows
  34.9 0.0 copy-start.1
  34.9 0.0 copy-start.2
  34.9 5.0 %far.1 = (f32[4,1024,1024]{2,1,0:T(8,128)S(1)}, f32[8,128]{1,0:T(8,128)}) custom-call(bf16[256,2048]{1,0:T(8,128)(2,1)S(1)} %join.1.rows, bf16[4,1024,2048]{2,1,0:T(8,128)(2,1)S(1)} %get-tuple-element.18.held, f32[4,1024,1024]{2,1,0:T(8,128)S(1)} %get-tuple-element.23._), custom_call_target="tpu_custom_call", output_to_operand_aliasing={{0}: (2, {})} | custom-call | flops 42949672960 | bytes 1048576 | tf_op jit(solution)/shard_map/far/pallas_call | solution.py:106
  39.9 2.6 %scores.1 = f32[1,64]{1,0:T(1,128)S(1)} custom-call(s32[16]{0:T(128)S(1)} %copy-done.1, s32[16]{0:T(128)S(1)} %copy-done.2, bf16[4,64,1024]{2,1,0:T(8,128)(2,1)S(1)} %stack.2.own, bf16[4,64,1024]{2,1,0:T(8,128)(2,1)S(1)} %collective-permute-done.4.ahead, bf16[4,64,1024]{2,1,0:T(8,128)(2,1)S(1)} %collective-permute-done.5.far, ...), custom_call_target="tpu_custom_call" | custom-call | flops 1073741824 | bytes 4194304 | tf_op jit(solution)/shard_map/scores/pallas_call | solution.py:217
  42.6 0.5 collective-permute-start.12
  43.1 0.8 %collective-permute-done.12 = f32[1,64]{1,0:T(1,128)S(1)} collective-permute-done((f32[1,64]{1,0:T(1,128)S(1)}, f32[1,64]{1,0:T(1,128)S(1)}, u32[]{:S(2)}, u32[]{:S(2)}) %collective-permute-start.12) | collective-permute-done | bytes 288 | tf_op jit(solution)/shard_map/ppermute | solution.py:230
  43.9 16.1 %all_to_all.5 = f32[64,1,64]{2,1,0:T(1,128)S(1)} all-to-all(f32[64,1,64]{2,1,0:T(1,128)S(1)} %broadcast_in_dim.9), channel_id=1, replica_groups={{0,1,2,3,4,5,6,7,8,9,10,11,12,13,14,15,32,33,34,35,36,37,38,39,40,41,42..., dimensions={0} | all-to-all | bytes 32768 | tf_op jit(solution)/shard_map/all_to_all | solution.py:232
  60.1 0.7 %reshape.8 = f32[4,16]{1,0:T(4,128)} reshape(f32[64]{0:T(128)S(1)} %reduce_sum.9) | data formatting | bytes 512 | tf_op jit(solution)/shard_map/reshape | solution.py:262
  (15 shorter events, 0.1 us)
Async XLA Ops:
  0.0 16.3 %copy-start = (bf16[64,1024]{1,0:T(8,128)(2,1)S(1)}, bf16[64,1024]{1,0:T(8,128)(2,1)}, u32[]{:S(2)}) copy-start(bf16[64,1024]{1,0:T(8,128)(2,1)} %refs_0_.1) | copy-start | bytes 393220
  0.0 7.4 %collective-permute-start.3 = (bf16[128,2048]{1,0:T(8,128)(2,1)}, bf16[128,2048]{1,0:T(8,128)(2,1)S(1)}, u32[]{:S(2)}, u32[]{:S(2)}) collective-permute-start(bf16[128,2048]{1,0:T(8,128)(2,1)} %own.1), channel_id=1, source_target_pairs={{0,16},{16,0},{32,48},{48,32},{64,80},{80,64},{96,112},{112,96},{1... | collective-permute-start | bytes 1572872 | tf_op jit(solution)/shard_map/ppermute | solution.py:240
  0.0 20.8 %collective-permute-start.7 = (bf16[128,2048]{1,0:T(8,128)(2,1)}, bf16[128,2048]{1,0:T(8,128)(2,1)S(1)}, u32[]{:S(2)}, u32[]{:S(2)}) collective-permute-start(bf16[128,2048]{1,0:T(8,128)(2,1)} %own.1), channel_id=1, source_target_pairs={{0,32},{16,48},{32,64},{48,80},{64,96},{80,112},{96,0},{112,16},{1... | collective-permute-start | bytes 1572872 | tf_op jit(solution)/shard_map/ppermute | solution.py:242
  1.7 19.1 %collective-permute-start.8 = (bf16[128,2048]{1,0:T(8,128)(2,1)}, bf16[128,2048]{1,0:T(8,128)(2,1)S(1)}, u32[]{:S(2)}, u32[]{:S(2)}) collective-permute-start(bf16[128,2048]{1,0:T(8,128)(2,1)} %own.1), channel_id=1, source_target_pairs={{0,96},{16,112},{32,0},{48,16},{64,32},{80,48},{96,64},{112,80},{1... | collective-permute-start | bytes 1572872 | tf_op jit(solution)/shard_map/ppermute | solution.py:243
  3.3 13.0 %collective-permute-start = (bf16[64,1024]{1,0:T(8,128)(2,1)}, bf16[64,1024]{1,0:T(8,128)(2,1)S(1)}, u32[]{:S(2)}, u32[]{:S(2)}) collective-permute-start(bf16[64,1024]{1,0:T(8,128)(2,1)} %refs_0_.1), channel_id=1, source_target_pairs={{0,3},{1,0},{2,1},{3,2},{4,7},{5,4},{6,5},{7,6},{8,11},{9,8},{10,9... | collective-permute-start | bytes 393224 | tf_op jit(solution)/shard_map/ppermute | solution.py:245
  7.4 8.8 %collective-permute-start.1 = (bf16[64,1024]{1,0:T(8,128)(2,1)}, bf16[64,1024]{1,0:T(8,128)(2,1)S(1)}, u32[]{:S(2)}, u32[]{:S(2)}) collective-permute-start(bf16[64,1024]{1,0:T(8,128)(2,1)} %refs_0_.1), channel_id=1, source_target_pairs={{0,2},{1,3},{2,0},{3,1},{4,6},{5,7},{6,4},{7,5},{8,10},{9,11},{10,... | collective-permute-start | bytes 393224 | tf_op jit(solution)/shard_map/ppermute | solution.py:245
  7.4 8.8 %collective-permute-start.2 = (bf16[64,1024]{1,0:T(8,128)(2,1)}, bf16[64,1024]{1,0:T(8,128)(2,1)S(1)}, u32[]{:S(2)}, u32[]{:S(2)}) collective-permute-start(bf16[64,1024]{1,0:T(8,128)(2,1)} %refs_0_.1), channel_id=1, source_target_pairs={{0,1},{1,2},{2,3},{3,0},{4,5},{5,6},{6,7},{7,4},{8,9},{9,10},{10,1... | collective-permute-start | bytes 393224 | tf_op jit(solution)/shard_map/ppermute | solution.py:245
  16.3 23.6 %collective-permute-start.4 = (bf16[4,64,1024]{2,1,0:T(8,128)(2,1)S(1)}, bf16[4,64,1024]{2,1,0:T(8,128)(2,1)S(1)}, u32[]{:S(2)}, u32[]{:S(2)}) collective-permute-start(bf16[4,64,1024]{2,1,0:T(8,128)(2,1)S(1)} %stack.2.own), channel_id=1, source_target_pairs={{0,12},{1,13},{2,14},{3,15},{4,0},{5,1},{6,2},{7,3},{8,4},{9,5},{1... | collective-permute-start | bytes 1572872 | tf_op jit(solution)/shard_map/ppermute | solution.py:249
  19.2 20.7 %collective-permute-start.5 = (bf16[4,64,1024]{2,1,0:T(8,128)(2,1)S(1)}, bf16[4,64,1024]{2,1,0:T(8,128)(2,1)S(1)}, u32[]{:S(2)}, u32[]{:S(2)}) collective-permute-start(bf16[4,64,1024]{2,1,0:T(8,128)(2,1)S(1)} %stack.2.own), channel_id=1, source_target_pairs={{0,8},{1,9},{2,10},{3,11},{4,12},{5,13},{6,14},{7,15},{8,0},{9,1},... | collective-permute-start | bytes 1572872 | tf_op jit(solution)/shard_map/ppermute | solution.py:249
  20.0 19.9 %collective-permute-start.6 = (bf16[4,64,1024]{2,1,0:T(8,128)(2,1)S(1)}, bf16[4,64,1024]{2,1,0:T(8,128)(2,1)S(1)}, u32[]{:S(2)}, u32[]{:S(2)}) collective-permute-start(bf16[4,64,1024]{2,1,0:T(8,128)(2,1)S(1)} %stack.2.own), channel_id=1, source_target_pairs={{0,4},{1,5},{2,6},{3,7},{4,8},{5,9},{6,10},{7,11},{8,12},{9,13},{1... | collective-permute-start | bytes 1572872 | tf_op jit(solution)/shard_map/ppermute | solution.py:249
  21.0 5.7 %collective-permute-start.10 = (bf16[256,2048]{1,0:T(8,128)(2,1)S(1)}, bf16[256,2048]{1,0:T(8,128)(2,1)S(1)}, u32[]{:S(2)}, u32[]{:S(2)}) collective-permute-start(bf16[256,2048]{1,0:T(8,128)(2,1)S(1)} %get-tuple-element.17.rows), channel_id=1, source_target_pairs={{0,16},{16,0},{32,48},{48,32},{64,80},{80,64},{96,112},{112,96},{1... | collective-permute-start | bytes 3145736 | tf_op jit(solution)/shard_map/ppermute | solution.py:240
  21.1 10.6 %collective-permute-start.9 = (bf16[128,2048]{1,0:T(8,128)(2,1)S(1)}, bf16[128,2048]{1,0:T(8,128)(2,1)S(1)}, u32[]{:S(2)}, u32[]{:S(2)}) collective-permute-start(bf16[128,2048]{1,0:T(8,128)(2,1)S(1)} %get-tuple-element.16), channel_id=1, source_target_pairs={{0,32},{16,112},{32,64},{48,16},{64,96},{80,48},{96,0},{112,80},{1... | collective-permute-start | bytes 1572872 | tf_op jit(solution)/shard_map/ppermute | solution.py:252
  31.7 3.1 %collective-permute-start.11 = (bf16[128,2048]{1,0:T(8,128)(2,1)S(1)}, bf16[128,2048]{1,0:T(8,128)(2,1)S(1)}, u32[]{:S(2)}, u32[]{:S(2)}) collective-permute-start(bf16[128,2048]{1,0:T(8,128)(2,1)S(1)} %bitcast.4), channel_id=1, source_target_pairs={{0,16},{16,0},{32,48},{48,32},{64,80},{80,64},{96,112},{112,96},{1... | collective-permute-start | bytes 1572872 | tf_op jit(solution)/shard_map/ppermute | solution.py:240
  34.9 5.0 %copy-start.1 = (s32[16]{0:T(128)S(1)}, s32[16]{0:T(128)}, u32[]{:S(2)}) copy-start(s32[16]{0:T(128)} %seq_start.1) | copy-start | bytes 196
  34.9 5.0 %copy-start.2 = (s32[16]{0:T(128)S(1)}, s32[16]{0:T(128)}, u32[]{:S(2)}) copy-start(s32[16]{0:T(128)} %seq_len.1) | copy-start | bytes 196
  42.6 1.3 %collective-permute-start.12 = (f32[1,64]{1,0:T(1,128)S(1)}, f32[1,64]{1,0:T(1,128)S(1)}, u32[]{:S(2)}, u32[]{:S(2)}) collective-permute-start(f32[1,64]{1,0:T(1,128)S(1)} %scores.1), channel_id=1, source_target_pairs={{0,16},{16,0},{32,48},{48,32},{64,80},{80,64},{96,112},{112,96},{1... | collective-permute-start | bytes 776 | tf_op jit(solution)/shard_map/ppermute | solution.py:230

commit v5 on v4

--- a/solution.py
+++ b/solution.py
@@ -253,10 +253,10 @@
 
     products, token = next_products("mid", [(3, 0), (1, 0)], pair, held, products, (0, nq))
     places = [(3, 1), (1, 1)]
-    products, token = next_products("other_low", places, pair_other, held, products, (0, nq // 2))
+    products, token = next_products("other_low", places, pair_other, held, products, (0, nq - 1))
     (far,) = stack([far], token)
     far_other = to_core(far)
-    products, token = next_products("other_high", places, pair_other, held, products, (nq // 2, nq))
+    products, token = next_products("other_high", places, pair_other, held, products, (nq - 1, nq))
     products, token = next_products("far", [(2, 0), (2, 1)], join(far, far_other), held, products, (0, nq))
     scores = partial_scores(seq_start, seq_len, acts, products)
     return total(scores).reshape(queries.shape[0], seq_start.shape[0])

time: 60.9 us -> 60.2 us (0.989)
  waiting for transfers between devices: 3.52 us -> 2.56 us
    ppermute x1, waiting for transfers between devices: 2.67 us -> 1.57 us  [on_device(): far = lax.ppermute(onward, 'row', Y_BY_CORE)]
  transfers between devices with their start and end apart: 13 -> 13, of which waited for: 2 -> 3; matrix products, arithmetic and copies ran while one was open for 0% -> 0% of each run, Pallas kernels for 38% -> 38%
where the time goes in v5:
time: 60.2 us; the launch traced here: 60.1 us
  Pallas kernels  25.6 us (43%)
  blocking collectives  16.5 us (27%)
  starting transfers between devices  14.6 us (24%)
  waiting for transfers between devices  2.56 us (4%)
  local copies, waits for them, and re-layouts  0.7 us (1%)
    all_to_all x1, blocking collectives, total(): lax.all_to_all(copies, ('row', 'col'), 0, 0, axis_index_groups=SAME_CORE,...  16.5 us
    pallas_call x4, Pallas kernels, next_products(): pl.pallas_call(functools.partial(next_kernel, places, computed), in_specs...  15.2 us
    pallas_call x1, Pallas kernels, near_products(): pl.pallas_call(functools.partial(near_kernel, places), in_specs=[HBM, VME...  7.54 us
    ppermute x3, starting transfers between devices, on_device(): lax.ppermute(activations, ('row', 'col'), along_both(along_z, along_x, -d))  5.42 us
    ppermute x3, starting transfers between devices, on_device(): lax.ppermute(own_act, ('row', 'col'), along_both(along_x, along_z, -d))  4.51 us
    pallas_call x1, Pallas kernels, partial_scores(): pl.pallas_call(score_kernel, in_specs=[SMEM] * 2 + [VMEM] * (len(acts) +...  2.65 us
    ppermute x1, starting transfers between devices, on_device(): below = lax.ppermute(out_grads, 'row', along_y(1))  1.72 us
    ppermute x1, waiting for transfers between devices, on_device(): far = lax.ppermute(onward, 'row', Y_BY_CORE)  1.57 us
  transfers between devices with their start and end apart: 13, of which 3 were waited for; matrix products, arithmetic and copies ran while one was open for 0% of the time, Pallas kernels for 38%

profile of v5, /device:TPU:0, one launch (start us, length us, event | category | flops | bytes accessed | tf_op | source)
XLA Modules:
  0.0 60.1 jit_solution(5142387065870205556)
XLA Ops:
  0.0 0.0 collective-permute-start.3
  0.0 1.7 %collective-permute-start.7 = (bf16[128,2048]{1,0:T(8,128)(2,1)}, bf16[128,2048]{1,0:T(8,128)(2,1)S(1)}, u32[]{:S(2)}, u32[]{:S(2)}) collective-permute-start(bf16[128,2048]{1,0:T(8,128)(2,1)} %own.1), channel_id=1, source_target_pairs={{0,32},{16,48},{32,64},{48,80},{64,96},{80,112},{96,0},{112,16},{1... | collective-permute-start | bytes 1572872 | tf_op jit(solution)/shard_map/ppermute | solution.py:242
  1.7 1.5 %collective-permute-start.8 = (bf16[128,2048]{1,0:T(8,128)(2,1)}, bf16[128,2048]{1,0:T(8,128)(2,1)S(1)}, u32[]{:S(2)}, u32[]{:S(2)}) collective-permute-start(bf16[128,2048]{1,0:T(8,128)(2,1)} %own.1), channel_id=1, source_target_pairs={{0,96},{16,112},{32,0},{48,16},{64,32},{80,48},{96,64},{112,80},{1... | collective-permute-start | bytes 1572872 | tf_op jit(solution)/shard_map/ppermute | solution.py:243
  3.3 4.2 %collective-permute-start = (bf16[64,1024]{1,0:T(8,128)(2,1)}, bf16[64,1024]{1,0:T(8,128)(2,1)S(1)}, u32[]{:S(2)}, u32[]{:S(2)}) collective-permute-start(bf16[64,1024]{1,0:T(8,128)(2,1)} %refs_0_.1), channel_id=1, source_target_pairs={{0,3},{1,0},{2,1},{3,2},{4,7},{5,4},{6,5},{7,6},{8,11},{9,8},{10,9... | collective-permute-start | bytes 393224 | tf_op jit(solution)/shard_map/ppermute | solution.py:245
  7.4 0.0 collective-permute-done.3.other
  7.4 1.3 %collective-permute-start.2 = (bf16[64,1024]{1,0:T(8,128)(2,1)}, bf16[64,1024]{1,0:T(8,128)(2,1)S(1)}, u32[]{:S(2)}, u32[]{:S(2)}) collective-permute-start(bf16[64,1024]{1,0:T(8,128)(2,1)} %refs_0_.1), channel_id=1, source_target_pairs={{0,1},{1,2},{2,3},{3,0},{4,5},{5,6},{6,7},{7,4},{8,9},{9,10},{10,1... | collective-permute-start | bytes 393224 | tf_op jit(solution)/shard_map/ppermute | solution.py:245
  8.7 7.5 %near.1 = (f32[4,1024,1024]{2,1,0:T(8,128)S(1)}, bf16[4,1024,2048]{2,1,0:T(8,128)(2,1)S(1)}, f32[8,128]{1,0:T(8,128)S(1)}) custom-call(bf16[128,2048]{1,0:T(8,128)(2,1)} %own.1, bf16[128,2048]{1,0:T(8,128)(2,1)S(1)} %collective-permute-done.3.other, bf16[4,1024,2048]{2,1,0:T(8,128)(2,1)} %queries.1), custom_call_target="tpu_custom_call" | custom-call | flops 42949672960 | bytes 16777216 | tf_op jit(solution)/shard_map/near/pallas_call | solution.py:83
  16.2 0.0 collective-permute-done.refs_1_
  16.3 0.0 collective-permute-done.1.refs_2_
  16.3 2.8 %collective-permute-start.4 = (bf16[4,64,1024]{2,1,0:T(8,128)(2,1)S(1)}, bf16[4,64,1024]{2,1,0:T(8,128)(2,1)S(1)}, u32[]{:S(2)}, u32[]{:S(2)}) collective-permute-start(bf16[4,64,1024]{2,1,0:T(8,128)(2,1)S(1)} %stack.2.own), channel_id=1, source_target_pairs={{0,12},{1,13},{2,14},{3,15},{4,0},{5,1},{6,2},{7,3},{8,4},{9,5},{1... | collective-permute-start | bytes 1572872 | tf_op jit(solution)/shard_map/ppermute | solution.py:249
  19.2 0.8 %collective-permute-start.5 = (bf16[4,64,1024]{2,1,0:T(8,128)(2,1)S(1)}, bf16[4,64,1024]{2,1,0:T(8,128)(2,1)S(1)}, u32[]{:S(2)}, u32[]{:S(2)}) collective-permute-start(bf16[4,64,1024]{2,1,0:T(8,128)(2,1)S(1)} %stack.2.own), channel_id=1, source_target_pairs={{0,8},{1,9},{2,10},{3,11},{4,12},{5,13},{6,14},{7,15},{8,0},{9,1},... | collective-permute-start | bytes 1572872 | tf_op jit(solution)/shard_map/ppermute | solution.py:249
  20.0 0.9 %collective-permute-start.6 = (bf16[4,64,1024]{2,1,0:T(8,128)(2,1)S(1)}, bf16[4,64,1024]{2,1,0:T(8,128)(2,1)S(1)}, u32[]{:S(2)}, u32[]{:S(2)}) collective-permute-start(bf16[4,64,1024]{2,1,0:T(8,128)(2,1)S(1)} %stack.2.own), channel_id=1, source_target_pairs={{0,4},{1,5},{2,6},{3,7},{4,8},{5,9},{6,10},{7,11},{8,12},{9,13},{1... | collective-permute-start | bytes 1572872 | tf_op jit(solution)/shard_map/ppermute | solution.py:249
  20.8 0.0 collective-permute-done.8.above
  20.9 0.1 pair.1
  21.0 0.1 collective-permute-start.10
  21.1 0.6 %collective-permute-start.9 = (bf16[128,2048]{1,0:T(8,128)(2,1)S(1)}, bf16[128,2048]{1,0:T(8,128)(2,1)S(1)}, u32[]{:S(2)}, u32[]{:S(2)}) collective-permute-start(bf16[128,2048]{1,0:T(8,128)(2,1)S(1)} %get-tuple-element.16), channel_id=1, source_target_pairs={{0,32},{16,112},{32,64},{48,16},{64,96},{80,48},{96,0},{112,80},{1... | collective-permute-start | bytes 1572872 | tf_op jit(solution)/shard_map/ppermute | solution.py:252
  21.7 5.0 %mid.1 = (f32[4,1024,1024]{2,1,0:T(8,128)S(1)}, f32[8,128]{1,0:T(8,128)}) custom-call(bf16[256,2048]{1,0:T(8,128)(2,1)S(1)} %get-tuple-element.17.rows, bf16[4,1024,2048]{2,1,0:T(8,128)(2,1)S(1)} %get-tuple-element.18.held, f32[4,1024,1024]{2,1,0:T(8,128)S(1)} %get-tuple-element.19._), custom_call_target="tpu_custom_call", output_to_operand_aliasing={{0}: (2, {})} | custom-call | flops 42949672960 | bytes 1048576 | tf_op jit(solution)/shard_map/mid/pallas_call | solution.py:106
  26.6 0.0 collective-permute-done.10.rows
  26.7 3.5 %other_low.1 = (f32[4,1024,1024]{2,1,0:T(8,128)S(1)}, f32[8,128]{1,0:T(8,128)S(1)}) custom-call(bf16[256,2048]{1,0:T(8,128)(2,1)S(1)} %collective-permute-done.10.rows, bf16[4,1024,2048]{2,1,0:T(8,128)(2,1)S(1)} %get-tuple-element.18.held, f32[4,1024,1024]{2,1,0:T(8,128)S(1)} %get-tuple-element.20._), custom_call_target="tpu_custom_call", output_to_operand_aliasing={{0}: (2, {})} | custom-call | flops 32212254720 | bytes 1048576 | tf_op jit(solution)/shard_map/other_low/pallas_call | solution.py:106
  30.1 1.6 %collective-permute-done.9.refs_0_ = bf16[128,2048]{1,0:T(8,128)(2,1)S(1)} collective-permute-done((bf16[128,2048]{1,0:T(8,128)(2,1)S(1)}, bf16[128,2048]{1,0:T(8,128)(2,1)S(1)}, u32[]{:S(2)}, u32[]{:S(2)}) %collective-permute-start.9) | collective-permute-done | bytes 524320 | tf_op jit(solution)/shard_map/ppermute | solution.py:252
  31.7 0.3 collective-permute-start.11
  32.1 1.8 %other_high.1 = (f32[4,1024,1024]{2,1,0:T(8,128)S(1)}, f32[8,128]{1,0:T(8,128)}) custom-call(bf16[256,2048]{1,0:T(8,128)(2,1)S(1)} %collective-permute-done.10.rows, bf16[4,1024,2048]{2,1,0:T(8,128)(2,1)S(1)} %get-tuple-element.18.held, f32[4,1024,1024]{2,1,0:T(8,128)S(1)} %get-tuple-element.22._), custom_call_target="tpu_custom_call", output_to_operand_aliasing={{0}: (2, {})} | custom-call | flops 10737418240 | bytes 1048576 | tf_op jit(solution)/shard_map/other_high/pallas_call | solution.py:106
  33.8 0.1 collective-permute-done.11.second
  33.9 0.1 join.1.rows
  34.0 0.0 copy-start.1
  34.0 0.0 copy-start.2
  34.0 5.0 %far.1 = (f32[4,1024,1024]{2,1,0:T(8,128)S(1)}, f32[8,128]{1,0:T(8,128)}) custom-call(bf16[256,2048]{1,0:T(8,128)(2,1)S(1)} %join.1.rows, bf16[4,1024,2048]{2,1,0:T(8,128)(2,1)S(1)} %get-tuple-element.18.held, f32[4,1024,1024]{2,1,0:T(8,128)S(1)} %get-tuple-element.23._), custom_call_target="tpu_custom_call", output_to_operand_aliasing={{0}: (2, {})} | custom-call | flops 42949672960 | bytes 1048576 | tf_op jit(solution)/shard_map/far/pallas_call | solution.py:106
  39.0 2.6 %scores.1 = f32[1,64]{1,0:T(1,128)S(1)} custom-call(s32[16]{0:T(128)S(1)} %copy-done.1, s32[16]{0:T(128)S(1)} %copy-done.2, bf16[4,64,1024]{2,1,0:T(8,128)(2,1)S(1)} %stack.2.own, bf16[4,64,1024]{2,1,0:T(8,128)(2,1)S(1)} %collective-permute-done.4.ahead, bf16[4,64,1024]{2,1,0:T(8,128)(2,1)S(1)} %collective-permute-done.5.far, ...), custom_call_target="tpu_custom_call" | custom-call | flops 1073741824 | bytes 4194304 | tf_op jit(solution)/shard_map/scores/pallas_call | solution.py:217
  41.7 0.4 collective-permute-start.12
  42.1 0.8 %collective-permute-done.12 = f32[1,64]{1,0:T(1,128)S(1)} collective-permute-done((f32[1,64]{1,0:T(1,128)S(1)}, f32[1,64]{1,0:T(1,128)S(1)}, u32[]{:S(2)}, u32[]{:S(2)}) %collective-permute-start.12) | collective-permute-done | bytes 288 | tf_op jit(solution)/shard_map/ppermute | solution.py:230
  42.9 16.5 %all_to_all.5 = f32[64,1,64]{2,1,0:T(1,128)S(1)} all-to-all(f32[64,1,64]{2,1,0:T(1,128)S(1)} %broadcast_in_dim.9), channel_id=1, replica_groups={{0,1,2,3,4,5,6,7,8,9,10,11,12,13,14,15,32,33,34,35,36,37,38,39,40,41,42..., dimensions={0} | all-to-all | bytes 32768 | tf_op jit(solution)/shard_map/all_to_all | solution.py:232
  59.4 0.7 %reshape.8 = f32[4,16]{1,0:T(4,128)} reshape(f32[64]{0:T(128)S(1)} %reduce_sum.9) | data formatting | bytes 512 | tf_op jit(solution)/shard_map/reshape | solution.py:262
  (15 shorter events, 0.1 us)
Async XLA Ops:
  0.0 16.3 %copy-start = (bf16[64,1024]{1,0:T(8,128)(2,1)S(1)}, bf16[64,1024]{1,0:T(8,128)(2,1)}, u32[]{:S(2)}) copy-start(bf16[64,1024]{1,0:T(8,128)(2,1)} %refs_0_.1) | copy-start | bytes 393220
  0.0 7.4 %collective-permute-start.3 = (bf16[128,2048]{1,0:T(8,128)(2,1)}, bf16[128,2048]{1,0:T(8,128)(2,1)S(1)}, u32[]{:S(2)}, u32[]{:S(2)}) collective-permute-start(bf16[128,2048]{1,0:T(8,128)(2,1)} %own.1), channel_id=1, source_target_pairs={{0,16},{16,0},{32,48},{48,32},{64,80},{80,64},{96,112},{112,96},{1... | collective-permute-start | bytes 1572872 | tf_op jit(solution)/shard_map/ppermute | solution.py:240
  0.0 20.8 %collective-permute-start.7 = (bf16[128,2048]{1,0:T(8,128)(2,1)}, bf16[128,2048]{1,0:T(8,128)(2,1)S(1)}, u32[]{:S(2)}, u32[]{:S(2)}) collective-permute-start(bf16[128,2048]{1,0:T(8,128)(2,1)} %own.1), channel_id=1, source_target_pairs={{0,32},{16,48},{32,64},{48,80},{64,96},{80,112},{96,0},{112,16},{1... | collective-permute-start | bytes 1572872 | tf_op jit(solution)/shard_map/ppermute | solution.py:242
  1.7 19.1 %collective-permute-start.8 = (bf16[128,2048]{1,0:T(8,128)(2,1)}, bf16[128,2048]{1,0:T(8,128)(2,1)S(1)}, u32[]{:S(2)}, u32[]{:S(2)}) collective-permute-start(bf16[128,2048]{1,0:T(8,128)(2,1)} %own.1), channel_id=1, source_target_pairs={{0,96},{16,112},{32,0},{48,16},{64,32},{80,48},{96,64},{112,80},{1... | collective-permute-start | bytes 1572872 | tf_op jit(solution)/shard_map/ppermute | solution.py:243
  3.3 13.0 %collective-permute-start = (bf16[64,1024]{1,0:T(8,128)(2,1)}, bf16[64,1024]{1,0:T(8,128)(2,1)S(1)}, u32[]{:S(2)}, u32[]{:S(2)}) collective-permute-start(bf16[64,1024]{1,0:T(8,128)(2,1)} %refs_0_.1), channel_id=1, source_target_pairs={{0,3},{1,0},{2,1},{3,2},{4,7},{5,4},{6,5},{7,6},{8,11},{9,8},{10,9... | collective-permute-start | bytes 393224 | tf_op jit(solution)/shard_map/ppermute | solution.py:245
  7.4 8.8 %collective-permute-start.1 = (bf16[64,1024]{1,0:T(8,128)(2,1)}, bf16[64,1024]{1,0:T(8,128)(2,1)S(1)}, u32[]{:S(2)}, u32[]{:S(2)}) collective-permute-start(bf16[64,1024]{1,0:T(8,128)(2,1)} %refs_0_.1), channel_id=1, source_target_pairs={{0,2},{1,3},{2,0},{3,1},{4,6},{5,7},{6,4},{7,5},{8,10},{9,11},{10,... | collective-permute-start | bytes 393224 | tf_op jit(solution)/shard_map/ppermute | solution.py:245
  7.4 8.8 %collective-permute-start.2 = (bf16[64,1024]{1,0:T(8,128)(2,1)}, bf16[64,1024]{1,0:T(8,128)(2,1)S(1)}, u32[]{:S(2)}, u32[]{:S(2)}) collective-permute-start(bf16[64,1024]{1,0:T(8,128)(2,1)} %refs_0_.1), channel_id=1, source_target_pairs={{0,1},{1,2},{2,3},{3,0},{4,5},{5,6},{6,7},{7,4},{8,9},{9,10},{10,1... | collective-permute-start | bytes 393224 | tf_op jit(solution)/shard_map/ppermute | solution.py:245
  16.3 22.7 %collective-permute-start.4 = (bf16[4,64,1024]{2,1,0:T(8,128)(2,1)S(1)}, bf16[4,64,1024]{2,1,0:T(8,128)(2,1)S(1)}, u32[]{:S(2)}, u32[]{:S(2)}) collective-permute-start(bf16[4,64,1024]{2,1,0:T(8,128)(2,1)S(1)} %stack.2.own), channel_id=1, source_target_pairs={{0,12},{1,13},{2,14},{3,15},{4,0},{5,1},{6,2},{7,3},{8,4},{9,5},{1... | collective-permute-start | bytes 1572872 | tf_op jit(solution)/shard_map/ppermute | solution.py:249
  19.2 19.9 %collective-permute-start.5 = (bf16[4,64,1024]{2,1,0:T(8,128)(2,1)S(1)}, bf16[4,64,1024]{2,1,0:T(8,128)(2,1)S(1)}, u32[]{:S(2)}, u32[]{:S(2)}) collective-permute-start(bf16[4,64,1024]{2,1,0:T(8,128)(2,1)S(1)} %stack.2.own), channel_id=1, source_target_pairs={{0,8},{1,9},{2,10},{3,11},{4,12},{5,13},{6,14},{7,15},{8,0},{9,1},... | collective-permute-start | bytes 1572872 | tf_op jit(solution)/shard_map/ppermute | solution.py:249
  20.0 19.1 %collective-permute-start.6 = (bf16[4,64,1024]{2,1,0:T(8,128)(2,1)S(1)}, bf16[4,64,1024]{2,1,0:T(8,128)(2,1)S(1)}, u32[]{:S(2)}, u32[]{:S(2)}) collective-permute-start(bf16[4,64,1024]{2,1,0:T(8,128)(2,1)S(1)} %stack.2.own), channel_id=1, source_target_pairs={{0,4},{1,5},{2,6},{3,7},{4,8},{5,9},{6,10},{7,11},{8,12},{9,13},{1... | collective-permute-start | bytes 1572872 | tf_op jit(solution)/shard_map/ppermute | solution.py:249
  21.0 5.7 %collective-permute-start.10 = (bf16[256,2048]{1,0:T(8,128)(2,1)S(1)}, bf16[256,2048]{1,0:T(8,128)(2,1)S(1)}, u32[]{:S(2)}, u32[]{:S(2)}) collective-permute-start(bf16[256,2048]{1,0:T(8,128)(2,1)S(1)} %get-tuple-element.17.rows), channel_id=1, source_target_pairs={{0,16},{16,0},{32,48},{48,32},{64,80},{80,64},{96,112},{112,96},{1... | collective-permute-start | bytes 3145736 | tf_op jit(solution)/shard_map/ppermute | solution.py:240
  21.1 10.6 %collective-permute-start.9 = (bf16[128,2048]{1,0:T(8,128)(2,1)S(1)}, bf16[128,2048]{1,0:T(8,128)(2,1)S(1)}, u32[]{:S(2)}, u32[]{:S(2)}) collective-permute-start(bf16[128,2048]{1,0:T(8,128)(2,1)S(1)} %get-tuple-element.16), channel_id=1, source_target_pairs={{0,32},{16,112},{32,64},{48,16},{64,96},{80,48},{96,0},{112,80},{1... | collective-permute-start | bytes 1572872 | tf_op jit(solution)/shard_map/ppermute | solution.py:252
  31.7 2.2 %collective-permute-start.11 = (bf16[128,2048]{1,0:T(8,128)(2,1)S(1)}, bf16[128,2048]{1,0:T(8,128)(2,1)S(1)}, u32[]{:S(2)}, u32[]{:S(2)}) collective-permute-start(bf16[128,2048]{1,0:T(8,128)(2,1)S(1)} %bitcast.4), channel_id=1, source_target_pairs={{0,16},{16,0},{32,48},{48,32},{64,80},{80,64},{96,112},{112,96},{1... | collective-permute-start | bytes 1572872 | tf_op jit(solution)/shard_map/ppermute | solution.py:240
  34.0 5.0 %copy-start.1 = (s32[16]{0:T(128)S(1)}, s32[16]{0:T(128)}, u32[]{:S(2)}) copy-start(s32[16]{0:T(128)} %seq_start.1) | copy-start | bytes 196
  34.0 5.0 %copy-start.2 = (s32[16]{0:T(128)S(1)}, s32[16]{0:T(128)}, u32[]{:S(2)}) copy-start(s32[16]{0:T(128)} %seq_len.1) | copy-start | bytes 196
  41.7 1.2 %collective-permute-start.12 = (f32[1,64]{1,0:T(1,128)S(1)}, f32[1,64]{1,0:T(1,128)S(1)}, u32[]{:S(2)}, u32[]{:S(2)}) collective-permute-start(f32[1,64]{1,0:T(1,128)S(1)} %scores.1), channel_id=1, source_target_pairs={{0,16},{16,0},{32,48},{48,32},{64,80},{80,64},{96,112},{112,96},{1... | collective-permute-start | bytes 776 | tf_op jit(solution)/shard_map/ppermute | solution.py:230
